TPU v7x, 32 devices: a whole 2x2x4 slice. The times are simulated.
32 devices in a mesh: orient: 8 (over y, x, core), pix: 4 (over z).
Axes of the slice: x: 2, y: 2, z: 4, core: 2. Of those that a mesh axis runs over, the one named last changes fastest.
Arguments:
- model: bfloat16 [6144, 65536], P('orient', 'pix'), may hold values from 0.012 to 3.32
- patterns: int32 [384, 65536], P(None, 'pix'), may hold values from 0 to 10, as said below
Outputs:
- updated: bfloat16 [6144, 65536], P('orient', 'pix')
Inputs may be any that keep to these rules, and one draw needn't show every extreme that they name: `patterns`: each pattern has a brightness level of its own; its counts are whole numbers from 0 to one less than that level.
All inputs are finite; a program needn't handle non-finite values.
Results may differ from a plain program's by a relative error of at most 0.0022.
Values may be sent and summed in bfloat16 or wider, within the bound.
No kernel may reach another device: no remote copies, remote signals or barrier semaphores. Data moves between devices by JAX's collectives and lax.ppermute only.
A program may use at most 128 MiB of HBM per device.

v0:
```python
import math

import jax
import jax.numpy as jnp
from jax import lax
from jax.sharding import PartitionSpec as P

PIX = 65536


prior_weight = 1.0


def normalize(scores):
    highest = jnp.max(scores, axis=0)
    overall = lax.pmax(highest, "orient")
    scaled = jnp.exp(scores - overall[None, :])
    exp_total = lax.psum(jnp.sum(scaled, axis=0), "orient")
    return (scaled / exp_total[None, :]).astype(jnp.bfloat16)


def on_device(model, patterns):
    anneal_beta = 2.0 / math.sqrt(PIX)
    counts = patterns.astype(jnp.float32)
    state = model
    intensity = state.astype(jnp.float32)
    log_slices = jnp.log(intensity)
    products = lax.dot_general(
        log_slices,
        counts,
        (((1,), (1,)), ((), ())),
        precision=lax.Precision.HIGHEST,
        preferred_element_type=jnp.float32,
    )
    local_totals = jnp.sum(intensity, axis=1)
    totals = lax.psum(local_totals, "pix")
    shares = lax.psum_scatter(products, "pix", scatter_dimension=1, tiled=True)
    likelihood = shares - totals[:, None]
    local_probs = normalize(anneal_beta * likelihood)
    probs = lax.all_gather(local_probs, "pix", axis=1, tiled=True)
    wide_probs = probs.astype(jnp.float32)
    numerator = jnp.dot(
        wide_probs, counts, precision=lax.Precision.HIGHEST, preferred_element_type=jnp.float32
    )
    normalizer = jnp.sum(wide_probs, axis=1)
    state = ((numerator + prior_weight * intensity) / (normalizer[:, None] + prior_weight)).astype(
        jnp.bfloat16
    )
    return state


def solution(mesh):
    placed = (P("orient", "pix"), P(None, "pix"))
    return jax.shard_map(
        on_device, mesh=mesh, in_specs=placed, out_specs=P("orient", "pix"), check_vma=False
    )
```

profile of v0, /device:TPU:0, one launch (start us, length us, event | category | flops | bytes accessed | tf_op | source)
XLA Modules:
  0.0 227.6 jit_solution(13038400167607533074)
XLA Ops:
  6.5 0.0 reduce-scatter.2.cloned.1.call-start
  6.5 86.0 %fusion = f32[768,384]{0,1:T(8,128)} fusion(bf16[768,16384]{1,0:T(8,128)(2,1)} %param.2, s32[384,16384]{1,0:T(8,128)} %param.3), kind=kOutput, calls=%fused_computation.3 | convolution fusion | flops 58000932864 | bytes 51511296 | tf_op jit(solution)/shard_map/dot_general | solution.py:28
  92.6 0.0 reduce-scatter.2.cloned.1.call-update
  92.6 10.0 %convert_reduce_fusion = f32[768]{0:T(1024)S(1)} fusion(bf16[768,16384]{1,0:T(8,128)(2,1)} %param.2), kind=kLoop, calls=%fused_computation.1 | loop fusion | flops 25165056 | bytes 25168896 | tf_op jit(solution)/shard_map/reduce_sum | solution.py:35
  102.6 14.0 %psum.14 = f32[768]{0:T(1024)S(1)} all-reduce(f32[768]{0:T(1024)S(1)} %convert_reduce_fusion), channel_id=1, replica_groups=mesh['orient'=8,'pix'=4] {'pix'}, use_global_device_ids=true, to_apply=%region_2.0 | all-reduce | flops 768 | bytes 6144 | tf_op jit(solution)/shard_map/psum | solution.py:36
  116.6 8.3 %reduce-scatter.2.cloned.1.call-done = f32[768,96]{0,1:T(8,128)} async-done(((f32[768,384]{0,1:T(8,128)}), f32[768,96]{0,1:T(8,128)}) %reduce-scatter.2.cloned.1.call-update) | async-done | bytes 294928 | tf_op jit(solution)/shard_map/reduce_scatter | solution.py:37
  124.9 1.1 fusion.5
  126.0 13.4 %pmax.7 = f32[96]{0:T(128)S(1)} all-reduce(f32[96]{0:T(128)S(1)} %fusion.5), channel_id=1, replica_groups=mesh['orient'=8,'pix'=4] {'orient'}, use_global_device_ids=true, to_apply=%region_4.0 | all-reduce | flops 96 | bytes 768 | tf_op jit(solution)/shard_map/pmax | solution.py:16
  139.4 1.2 fusion.6
  140.6 11.8 %psum.15 = f32[96]{0:T(128)S(1)} all-reduce(f32[96]{0:T(128)S(1)} %fusion.6), channel_id=1, replica_groups=mesh['orient'=8,'pix'=4] {'orient'}, use_global_device_ids=true, to_apply=%region_6.0 | all-reduce | flops 96 | bytes 768 | tf_op jit(solution)/shard_map/psum | solution.py:18
  152.4 1.1 divide_convert_fusion
  153.5 16.8 %all_gather.3 = bf16[768,384]{0,1:T(8,128)(2,1)S(1)} all-gather(bf16[768,96]{0,1:T(8,128)(2,1)S(1)} %divide_convert_fusion), channel_id=1, replica_groups=mesh['orient'=8,'pix'=4] {'pix'}, dimensions={1}, use_global_device_ids=true | all-gather | bytes 737280 | tf_op jit(solution)/shard_map/all_gather | solution.py:40
  170.3 0.1 convert_reduce_fusion.1
  170.4 50.3 %fusion.2 = bf16[768,16384]{1,0:T(8,128)(2,1)} fusion(bf16[768,16384]{1,0:T(8,128)(2,1)} %param.2, bf16[768,384]{0,1:T(8,128)(2,1)S(1)} %all_gather.3, f32[768]{0:T(1024)S(1)} %broadcast_add_fusion, s32[384,16384]{1,0:T(8,128)} %param.3), kind=kOutput, calls=%fused_computation.5 | convolution fusion | flops 58038681600 | bytes 76090368 | tf_op jit(solution)/shard_map/dot_general | solution.py:42
  (1 shorter events, 0.0 us)
Async XLA Ops:
  6.5 118.4 %reduce-scatter.2.cloned.1.call-start = ((), (), s32[]{:S(2)}) async-start(), calls=%async_computation.1 | async-start | bytes 1474560 | tf_op jit(solution)/shard_map/reduce_scatter | solution.py:37
Sparse Core Ops, SparseCore 0:
  92.7 32.1 reduce-scatter.1
where the time goes:
time: 228 us
  matrix products  136 us (60%)
  blocking collectives  56 us (25%)
  other arithmetic  13.5 us (6%)
  between operations  13.4 us (6%)
  waiting for transfers between devices  8.36 us (4%)
    dot_general x1, matrix products, on_device(): lax.dot_general(log_slices, counts, (((1,), (1,)), ((), ())), precision=l...  86 us
    dot_general x1, matrix products, on_device(): jnp.dot(wide_probs, counts, precision=lax.Precision.HIGHEST, preferred_el...  50.3 us
    all_gather x1, blocking collectives, on_device(): probs = lax.all_gather(local_probs, 'pix', axis=1, tiled=True)  16.8 us
    psum x1, blocking collectives, on_device(): totals = lax.psum(local_totals, 'pix')  14 us
    pmax x1, blocking collectives, normalize(): overall = lax.pmax(highest, 'orient')  13.4 us
    psum x1, blocking collectives, normalize(): exp_total = lax.psum(jnp.sum(scaled, axis=0), 'orient')  11.8 us
    reduce_sum x1, other arithmetic, on_device(): local_totals = jnp.sum(intensity, axis=1)  9.98 us
    reduce_scatter x1, waiting for transfers between devices, on_device(): shares = lax.psum_scatter(products, 'pix', scatter_dimension=1, tiled=True)  8.35 us
  transfers between devices with their start and end apart: 1, of which 1 were waited for; matrix products, arithmetic and copies ran while one was open for 4% of the time, Pallas kernels for 0%

commit v1 on v0

v1 whole, which is shorter than its diff:
```python
import functools
import math

import jax
import jax.numpy as jnp
from jax import lax
from jax.experimental import pallas as pl
from jax.experimental.pallas import tpu as pltpu
from jax.sharding import PartitionSpec as P

f32 = jnp.float32
bf16 = jnp.bfloat16
MIB = 1 << 20
PRIOR = 1.0
STEP = 1024
TILE = 256
AHEAD = 3


def params(mib):
    return pltpu.CompilerParams(vmem_limit_bytes=mib * MIB)


def accumulate(model, counts, accs, totals, px, tiles):
    lhs = counts[:, px]
    for n in range(tiles):
        rows = slice(n * TILE, (n + 1) * TILE)
        x = model[rows, px].astype(f32)
        logs = jnp.log(x)
        upper = logs.astype(bf16)
        rest = (logs - upper.astype(f32)).astype(bf16)
        slot = n % 2
        pltpu.matmul_push_rhs(upper, slot, 0, transpose=True)
        pltpu.matmul_push_rhs(rest, slot, 1, transpose=True)
        pltpu.matmul_acc_lhs(accs[2 * n], lhs, load_staged_rhs=slot)
        pltpu.matmul_acc_lhs(accs[2 * n + 1], lhs, load_staged_rhs=slot)
        totals[rows, :] += x[:, :128] + x[:, 128:]


def finish(accs, totals, whole, shares, tiles, place):
    for n in range(tiles):
        rows = slice(n * TILE, (n + 1) * TILE)
        total = jnp.sum(totals[rows, :].T, axis=0, keepdims=True)
        whole[:, rows] = pltpu.matmul_pop(accs[2 * n]) + pltpu.matmul_pop(accs[2 * n + 1]) - total
    count = len(shares)
    depth = whole.shape[0] // count
    for k in range(count):
        owner = lax.rem(place + k, count)
        shares[k][...] = whole[pl.ds(pl.multiple_of(owner * depth, 8), depth), :]


def score_kernel(count, first, row, place_ref, model_hbm, *refs):
    if first:
        patterns_hbm, refs = refs[0], refs[1:]
    else:
        counts, refs = refs[0], refs[1:]
    shares, refs = refs[:count], refs[count:]
    model, refs = refs[0], refs[1:]
    if first:
        counts, refs = refs[0], refs[1:]
        raw, raw_sems, refs = refs[0], refs[1], refs[2:]
    whole, totals, model_sems = refs
    rows, pixels = model.shape
    frames = counts.shape[0]
    steps = pixels // STEP
    tiles = rows // TILE
    totals[...] = jnp.zeros_like(totals)

    def window(i):
        return pl.ds(pl.multiple_of(i * STEP, STEP), STEP)

    def model_copy(i):
        return pltpu.make_async_copy(
            model_hbm.at[pl.ds(row, rows), window(i)], model.at[:, window(i)], model_sems.at[i]
        )

    def raw_copy(i):
        slot = lax.rem(i, AHEAD)
        return pltpu.make_async_copy(patterns_hbm.at[:, window(i)], raw.at[slot], raw_sems.at[slot])

    for i in range(AHEAD):
        model_copy(i).start()
        if first:
            raw_copy(i).start()

    def scoped(*accs):
        @pl.loop(0, steps)
        def _(i):
            model_copy(i).wait()
            if first:
                raw_copy(i).wait()
                counts[:, window(i)] = raw[lax.rem(i, AHEAD)].astype(f32).astype(bf16)

            @pl.when(i + AHEAD < steps)
            def _():
                model_copy(i + AHEAD).start()
                if first:
                    raw_copy(i + AHEAD).start()

            for q in range(STEP // TILE):
                px = pl.ds(pl.multiple_of(i * STEP + q * TILE, TILE), TILE)
                accumulate(model, counts, accs, totals, px, tiles)

        finish(accs, totals, whole, shares, tiles, place_ref[0])

    pl.run_scoped(scoped, *[pltpu.ACC(j % 2)((frames, TILE), f32) for j in range(2 * tiles)])


def partial_scores(place, model, patterns, counts, row, rows, pix_count):
    pixels = model.shape[1]
    first = counts is None
    frames = patterns.shape[0]
    steps = pixels // STEP
    whole_vmem = pl.BlockSpec(memory_space=pltpu.VMEM)
    anywhere = pl.BlockSpec(memory_space=pl.ANY)
    if first:
        operands = (place, model, patterns)
        in_specs = [pl.BlockSpec(memory_space=pltpu.SMEM), anywhere, anywhere]
    else:
        operands = (place, model, pltpu.with_memory_space_constraint(counts, pltpu.VMEM))
        in_specs = [pl.BlockSpec(memory_space=pltpu.SMEM), anywhere, whole_vmem]
    out_shape = [jax.ShapeDtypeStruct((frames // pix_count, rows), f32)] * pix_count
    out_shape.append(pltpu.VMEM((rows, pixels), bf16))
    scratch = []
    if first:
        out_shape.append(pltpu.VMEM((frames, pixels), bf16))
        scratch += [pltpu.VMEM((AHEAD, frames, STEP), jnp.int32), pltpu.SemaphoreType.DMA((AHEAD,))]
    scratch += [
        pltpu.VMEM((frames, rows), f32),
        pltpu.VMEM((rows, 128), f32),
        pltpu.SemaphoreType.DMA((steps,)),
    ]
    return pl.pallas_call(
        functools.partial(score_kernel, pix_count, first, row),
        out_shape=out_shape,
        in_specs=in_specs,
        out_specs=[whole_vmem] * len(out_shape),
        scratch_shapes=scratch,
        compiler_params=params(14),
        cost_estimate=pl.CostEstimate(
            flops=4 * rows * pixels * frames,
            bytes_accessed=2 * rows * pixels + (4 * frames * pixels if first else 0),
            transcendentals=rows * pixels,
        ),
    )(*operands)


def stats_kernel(beta, groups, *refs):
    scores, stat = refs[-2:]
    at = 0
    start = 0
    for size in groups:
        parts = refs[at : at + size]
        at += size
        total = parts[0][...]
        for part in parts[1:]:
            total = total + part[...]
        scores[:, start : start + total.shape[1]] = total * beta
        start += total.shape[1]
    values = scores[...]
    highest = jnp.max(values, axis=1, keepdims=True)
    sums = jnp.sum(jnp.exp(values - highest), axis=1, keepdims=True)
    lane = lax.broadcasted_iota(jnp.int32, stat.shape, 1)
    stat[...] = jnp.where(lane == 0, highest, sums)


def probs_kernel(scores, stats, probs):
    highest = stats[:, :, 0:1]
    overall = jnp.max(highest, axis=0)
    total = jnp.sum(stats[:, :, 1:2] * jnp.exp(highest - overall[None]), axis=0)
    probs[...] = (jnp.exp(scores[...] - overall) / total).astype(bf16)


def update_kernel(count, places, place_ref, *refs):
    shares, refs = refs[:count], refs[count:]
    counts, refs = refs[0], refs[1:]
    models, refs = refs[:places], refs[places:]
    out, turned, probs, inverse = refs
    step = pl.program_id(0)
    depth = shares[0].shape[0]
    frames = depth * count
    wide = probs.shape[1]

    @pl.when(step == 0)
    def _():
        turned[frames:, :] = jnp.zeros((wide - frames, turned.shape[1]), f32)
        for k in range(count):
            owner = lax.rem(place_ref[0] + count - k, count)
            turned[pl.ds(pl.multiple_of(owner * depth, 8), depth), :] = shares[k][...].astype(f32)
        across = turned[...].T
        probs[...] = across.astype(bf16)
        inverse[...] = 1.0 / (jnp.sum(across, axis=1, keepdims=True) + PRIOR)

    width = out.shape[1]

    def scoped(*accs):
        for q in range(width // TILE):
            px = pl.ds(pl.multiple_of(step * width + q * TILE, TILE), TILE)
            unit = q % 2
            for k in range(wide // TILE):
                part = counts[k * TILE : min((k + 1) * TILE, frames), px]
                if part.shape[0] < TILE:
                    part = jnp.concatenate([part, jnp.zeros((TILE - part.shape[0], TILE), bf16)], 0)
                pltpu.matmul_push_rhs(part, k % 2, unit)
                pltpu.matmul_acc_lhs(accs[unit], probs[:, k * TILE : (k + 1) * TILE], load_staged_rhs=k % 2)
            numerator = pltpu.matmul_pop(accs[unit])
            at = 0
            for model in models:
                rows = slice(at, at + model.shape[0])
                at += model.shape[0]
                out[rows, q * TILE : (q + 1) * TILE] = (
                    (numerator[rows] + model[:, px].astype(f32)) * inverse[rows, :]
                ).astype(bf16)

    pl.run_scoped(scoped, *[pltpu.ACC(j)((out.shape[0], TILE), f32) for j in range(2)])


def update(place, shares, counts, models):
    frames, pixels = counts.shape
    rows = sum(m.shape[0] for m in models)
    wide = -(-frames // TILE) * TILE
    whole_vmem = pl.BlockSpec(memory_space=pltpu.VMEM)
    pinned = [pltpu.with_memory_space_constraint(a, pltpu.VMEM) for a in (counts, *models)]
    return pl.pallas_call(
        functools.partial(update_kernel, len(shares), len(models)),
        out_shape=jax.ShapeDtypeStruct((rows, pixels), bf16),
        grid=(pixels // STEP,),
        in_specs=[pl.BlockSpec(memory_space=pltpu.SMEM)] + [whole_vmem] * (len(shares) + len(pinned)),
        out_specs=pl.BlockSpec((rows, STEP), lambda i: (0, i)),
        scratch_shapes=[
            pltpu.VMEM((wide, rows), f32),
            pltpu.VMEM((rows, wide), bf16),
            pltpu.VMEM((rows, 1), f32),
        ],
        compiler_params=params(16),
        cost_estimate=pl.CostEstimate(
            flops=2 * rows * pixels * frames, bytes_accessed=2 * rows * pixels, transcendentals=0
        ),
    )(place, *shares, *pinned)


def shift(x, k, count):
    return lax.ppermute(x, "pix", [(i, (i + k) % count) for i in range(count)])


def on_device(pix_count, orient_count, beta, model, patterns):
    place = lax.axis_index("pix").astype(jnp.int32).reshape(1)
    rows = model.shape[0]
    head = max(TILE, rows // 3 * 2 // TILE * TILE)
    first = partial_scores(place, model, patterns, None, 0, head, pix_count)
    counts = first[-1]
    second = partial_scores(place, model, patterns, counts, head, rows - head, pix_count)
    pieces, groups = [], []
    for result in (first, second):
        pieces.append(result[0])
        pieces += [shift(result[k], k, pix_count) for k in range(1, pix_count)]
        groups.append(pix_count)
    depth = patterns.shape[0] // pix_count
    scores, stat = pl.pallas_call(
        functools.partial(stats_kernel, beta, tuple(groups)),
        out_shape=[jax.ShapeDtypeStruct((depth, rows), f32), jax.ShapeDtypeStruct((depth, 128), f32)],
        compiler_params=params(14),
    )(*pieces)
    stats = lax.all_gather(stat, "orient")
    probs = pl.pallas_call(
        probs_kernel,
        out_shape=jax.ShapeDtypeStruct((depth, rows), bf16),
        compiler_params=params(14),
    )(scores, stats)
    shares = [probs] + [shift(probs, k, pix_count) for k in range(1, pix_count)]
    return update(place, shares, counts, [first[-2], second[-1]])


def solution(mesh):
    placed = (P("orient", "pix"), P(None, "pix"))

    def run(model, patterns):
        beta = 2.0 / math.sqrt(model.shape[1])
        body = functools.partial(on_device, mesh.shape["pix"], mesh.shape["orient"], beta)
        with jax.sharding.use_abstract_mesh(mesh.abstract_mesh):
            return jax.shard_map(
                body, mesh=mesh, in_specs=placed, out_specs=P("orient", "pix"), check_vma=False
            )(model, patterns)

    return run
```

time: 228 us -> 125 us (0.55)
  matrix products: 136 us -> 0 us
  Pallas kernels: 0 us -> 47.4 us
  blocking collectives: 56 us -> 9.6 us
  waiting for transfers between devices: 8.36 us -> 31.7 us
  local copies, waits for them, and re-layouts: 0 us -> 21 us
  starting transfers between devices: 0.01 us -> 15 us
  other arithmetic: 13.5 us -> 0 us
  between operations: 13.4 us -> 0.06 us
    dot_general x2 -> x0, matrix products: 136 us -> none  [the longest x1 86 us: on_device(): lax.dot_general(log_slices, counts, (((1,), (1,)), ((), ())), precision=l...]
    pallas_call x0 -> x5, Pallas kernels: none -> 47.4 us  [the longest x2 27.6 us: partial_scores(): pl.pallas_call(functools.partial(score_kernel, pix_count, first, row), ou...]
    ppermute x0 -> x9, waiting for transfers between devices: none -> 31.7 us  [shift(): return lax.ppermute(x, 'pix', [(i, (i + k) % count) for i in range(count)])]
    psum x2 -> x0, blocking collectives: 25.8 us -> none  [the longest x1 14 us: on_device(): totals = lax.psum(local_totals, 'pix')]
    unnamed x0 -> x8, local copies, waits for them, and re-layouts: none -> 21 us
    ppermute x0 -> x9, starting transfers between devices: none -> 15 us  [shift(): return lax.ppermute(x, 'pix', [(i, (i + k) % count) for i in range(count)])]
    pmax x1 -> x0, blocking collectives: 13.4 us -> none  [normalize(): overall = lax.pmax(highest, 'orient')]
    reduce_sum x3 -> x0, other arithmetic: 11.3 us -> none  [the longest x1 9.98 us: on_device(): local_totals = jnp.sum(intensity, axis=1)]
  transfers between devices with their start and end apart: 1 -> 9, of which waited for: 1 -> 3; matrix products, arithmetic and copies ran while one was open for 4% -> 0% of each run, Pallas kernels for 0% -> 0%
where the time goes in v1:
time: 125 us
  Pallas kernels  47.4 us (38%)
  waiting for transfers between devices  31.7 us (25%)
  local copies, waits for them, and re-layouts  21 us (17%)
  starting transfers between devices  15 us (12%)
  blocking collectives  9.6 us (8%)
    ppermute x9, waiting for transfers between devices, shift(): return lax.ppermute(x, 'pix', [(i, (i + k) % count) for i in range(count)])  31.7 us
    pallas_call x2, Pallas kernels, partial_scores(): pl.pallas_call(functools.partial(score_kernel, pix_count, first, row), ou...  27.6 us
    unnamed x8, local copies, waits for them, and re-layouts  21 us
    pallas_call x1, Pallas kernels, update(): pl.pallas_call(functools.partial(update_kernel, len(shares), len(models))...  19.3 us
    ppermute x9, starting transfers between devices, shift(): return lax.ppermute(x, 'pix', [(i, (i + k) % count) for i in range(count)])  15 us
    all_gather x1, blocking collectives, on_device(): stats = lax.all_gather(stat, 'orient')  9.6 us
  transfers between devices with their start and end apart: 9, of which 3 were waited for; matrix products, arithmetic and copies ran while one was open for 0% of the time, Pallas kernels for 0%

profile of v1, /device:TPU:0, one launch (start us, length us, event | category | flops | bytes accessed | tf_op | source)
XLA Modules:
  0.0 124.8 jit_solution(10336237914891781712)
XLA Ops:
  0.0 17.8 %shard_map.28 = (f32[96,512]{1,0:T(8,128)S(1)}, f32[96,512]{1,0:T(8,128)S(1)}, f32[96,512]{1,0:T(8,128)S(1)}, f32[96,512]{1,0:T(8,128)S(1)}, bf16[512,16384]{1,0...) custom-call(s32[1]{0:T(128)} %bitcast.place_ref, bf16[768,16384]{1,0:T(8,128)(2,1)} %model_hbm.3, s32[384,16384]{1,0:T(8,128)} %refs_0_.1), custom_call_target="tpu_custom_call" | custom-call | flops 12884901888 | bytes 41943040 | tf_op jit(solution)/shard_map/pallas_call | solution.py:133
  17.8 0.0 copy-start.2
  17.9 6.2 %copy-done.2 = bf16[512,16384]{1,0:T(8,128)(2,1)} copy-done((bf16[512,16384]{1,0:T(8,128)(2,1)}, bf16[512,16384]{1,0:T(8,128)(2,1)S(1)}, u32[]{:S(2)}) %copy-start.2) | copy-done | bytes 16777240
  24.0 9.8 %shard_map.29 = (f32[96,256]{1,0:T(8,128)S(1)}, f32[96,256]{1,0:T(8,128)S(1)}, f32[96,256]{1,0:T(8,128)S(1)}, f32[96,256]{1,0:T(8,128)S(1)}, bf16[256,16384]{1,0:T(8,128)(2,1)S(1)}) custom-call(s32[1]{0:T(128)} %bitcast.place_ref, bf16[768,16384]{1,0:T(8,128)(2,1)} %model_hbm.3, bf16[384,16384]{1,0:T(8,128)(2,1)S(1)} %get-tuple-element.22.refs_0_.refs_4_), custom_call_target="tpu_custom_call" | custom-call | flops 6442450944 | bytes 8388608 | tf_op jit(solution)/shard_map/pallas_call | solution.py:133
  33.8 0.0 copy-start
  33.8 4.5 %copy-done = bf16[384,16384]{1,0:T(8,128)(2,1)} copy-done((bf16[384,16384]{1,0:T(8,128)(2,1)}, bf16[384,16384]{1,0:T(8,128)(2,1)S(1)}, u32[]{:S(2)}) %copy-start) | copy-done | bytes 12582936
  38.3 3.0 %collective-permute-start.3 = (f32[96,256]{1,0:T(8,128)S(1)}, f32[96,256]{1,0:T(8,128)S(1)}, u32[]{:S(2)}, u32[]{:S(2)}) collective-permute-start(f32[96,256]{1,0:T(8,128)S(1)} %get-tuple-element.24), channel_id=1, source_target_pairs={{0,1},{1,2},{2,3},{3,0},{4,5},{5,6},{6,7},{7,4},{8,9},{9,10},{10,1... | collective-permute-start | bytes 294920 | tf_op jit(solution)/shard_map/ppermute | solution.py:243
  41.3 1.6 %collective-permute-start = (f32[96,512]{1,0:T(8,128)S(1)}, f32[96,512]{1,0:T(8,128)S(1)}, u32[]{:S(2)}, u32[]{:S(2)}) collective-permute-start(f32[96,512]{1,0:T(8,128)S(1)} %get-tuple-element.19), channel_id=1, source_target_pairs={{0,1},{1,2},{2,3},{3,0},{4,5},{5,6},{6,7},{7,4},{8,9},{9,10},{10,1... | collective-permute-start | bytes 589832 | tf_op jit(solution)/shard_map/ppermute | solution.py:243
  42.9 1.0 collective-permute-start.1
  43.9 2.9 %collective-permute-start.2 = (f32[96,512]{1,0:T(8,128)S(1)}, f32[96,512]{1,0:T(8,128)S(1)}, u32[]{:S(2)}, u32[]{:S(2)}) collective-permute-start(f32[96,512]{1,0:T(8,128)S(1)} %get-tuple-element.21), channel_id=1, source_target_pairs={{0,3},{1,0},{2,1},{3,2},{4,7},{5,4},{6,5},{7,6},{8,11},{9,8},{10,9... | collective-permute-start | bytes 589832 | tf_op jit(solution)/shard_map/ppermute | solution.py:243
  46.8 0.3 collective-permute-start.4
  47.2 0.0 collective-permute-done.3.refs_5_
  47.2 1.9 %collective-permute-start.5 = (f32[96,256]{1,0:T(8,128)S(1)}, f32[96,256]{1,0:T(8,128)S(1)}, u32[]{:S(2)}, u32[]{:S(2)}) collective-permute-start(f32[96,256]{1,0:T(8,128)S(1)} %get-tuple-element.26), channel_id=1, source_target_pairs={{0,3},{1,0},{2,1},{3,2},{4,7},{5,4},{6,5},{7,6},{8,11},{9,8},{10,9... | collective-permute-start | bytes 294920 | tf_op jit(solution)/shard_map/ppermute | solution.py:243
  49.0 18.4 %collective-permute-done.4.refs_6_ = f32[96,256]{1,0:T(8,128)S(1)} collective-permute-done((f32[96,256]{1,0:T(8,128)S(1)}, f32[96,256]{1,0:T(8,128)S(1)}, u32[]{:S(2)}, u32[]{:S(2)}) %collective-permute-start.4) | collective-permute-done | bytes 98336 | tf_op jit(solution)/shard_map/ppermute | solution.py:243
  67.4 0.0 collective-permute-done.5.refs_7_
  67.4 0.0 collective-permute-done.refs_1_
  67.4 0.0 collective-permute-done.1.refs_2_
  67.4 0.0 collective-permute-done.2.refs_3_
  67.4 0.2 shard_map.30
  67.6 9.6 %all-gather = f32[768,128]{1,0:T(8,128)S(1)} all-gather(f32[96,128]{1,0:T(8,128)S(1)} %get-tuple-element.28), channel_id=2, replica_groups=mesh['orient'=8,'pix'=4] {'orient'}, dimensions={0}, use_global_device_ids=true | all-gather | bytes 442368 | tf_op jit(solution)/shard_map/all_gather | solution.py:264
  77.2 0.3 shard_map.31.refs_0_
  77.5 3.7 %collective-permute-start.8 = (bf16[96,768]{1,0:T(8,128)(2,1)S(1)}, bf16[96,768]{1,0:T(8,128)(2,1)S(1)}, u32[]{:S(2)}, u32[]{:S(2)}) collective-permute-start(bf16[96,768]{1,0:T(8,128)(2,1)S(1)} %shard_map.31.refs_0_), channel_id=1, source_target_pairs={{0,3},{1,0},{2,1},{3,2},{4,7},{5,4},{6,5},{7,6},{8,11},{9,8},{10,9... | collective-permute-start | bytes 442376 | tf_op jit(solution)/shard_map/ppermute | solution.py:243
  81.2 0.4 collective-permute-start.7
  81.6 0.2 collective-permute-start.6
  81.8 3.6 %collective-permute-done.8.refs_3_ = bf16[96,768]{1,0:T(8,128)(2,1)S(1)} collective-permute-done((bf16[96,768]{1,0:T(8,128)(2,1)S(1)}, bf16[96,768]{1,0:T(8,128)(2,1)S(1)}, u32[]{:S(2)}, u32[]{:S(2)}) %collective-permute-start.8) | collective-permute-done | bytes 147488 | tf_op jit(solution)/shard_map/ppermute | solution.py:243
  85.5 9.7 %collective-permute-done.7.refs_2_ = bf16[96,768]{1,0:T(8,128)(2,1)S(1)} collective-permute-done((bf16[96,768]{1,0:T(8,128)(2,1)S(1)}, bf16[96,768]{1,0:T(8,128)(2,1)S(1)}, u32[]{:S(2)}, u32[]{:S(2)}) %collective-permute-start.7) | collective-permute-done | bytes 147488 | tf_op jit(solution)/shard_map/ppermute | solution.py:243
  95.2 0.0 collective-permute-done.6.refs_1_
  95.2 0.0 copy-start.1
  95.2 4.6 %copy-done.1 = bf16[384,16384]{1,0:T(8,128)(2,1)S(1)} copy-done((bf16[384,16384]{1,0:T(8,128)(2,1)S(1)}, bf16[384,16384]{1,0:T(8,128)(2,1)}, u32[]{:S(2)}) %copy-start.1) | copy-done | bytes 12582936
  99.8 0.0 copy-start.3
  99.8 5.8 %copy-done.3 = bf16[512,16384]{1,0:T(8,128)(2,1)S(1)} copy-done((bf16[512,16384]{1,0:T(8,128)(2,1)S(1)}, bf16[512,16384]{1,0:T(8,128)(2,1)}, u32[]{:S(2)}) %copy-start.3) | copy-done | bytes 16777240
  105.5 19.3 %shard_map.32 = bf16[768,16384]{1,0:T(8,128)(2,1)} custom-call(s32[1]{0:T(128)} %bitcast.place_ref, bf16[96,768]{1,0:T(8,128)(2,1)S(1)} %shard_map.31.refs_0_, bf16[96,768]{1,0:T(8,128)(2,1)S(1)} %collective-permute-done.6.refs_1_, bf16[96,768]{1,0:T(8,128)(2,1)S(1)} %collective-permute-done.7.refs_2_, bf16[96,768]{1,0:T(8,128)(2,1)S(1)} %collective-permute-done.8.refs_3_, ...), custom_call_target="tpu_custom_call" | custom-call | flops 9663676416 | bytes 25165824 | tf_op jit(solution)/shard_map/pallas_call | solution.py:224
Async XLA Ops:
  17.8 6.2 %copy-start.2 = (bf16[512,16384]{1,0:T(8,128)(2,1)}, bf16[512,16384]{1,0:T(8,128)(2,1)S(1)}, u32[]{:S(2)}) copy-start(bf16[512,16384]{1,0:T(8,128)(2,1)S(1)} %get-tuple-element.29.refs_5_) | copy-start | bytes 50331652
  33.8 4.5 %copy-start = (bf16[384,16384]{1,0:T(8,128)(2,1)}, bf16[384,16384]{1,0:T(8,128)(2,1)S(1)}, u32[]{:S(2)}) copy-start(bf16[384,16384]{1,0:T(8,128)(2,1)S(1)} %get-tuple-element.22.refs_0_.refs_4_) | copy-start | bytes 37748740
  38.3 8.9 %collective-permute-start.3 = (f32[96,256]{1,0:T(8,128)S(1)}, f32[96,256]{1,0:T(8,128)S(1)}, u32[]{:S(2)}, u32[]{:S(2)}) collective-permute-start(f32[96,256]{1,0:T(8,128)S(1)} %get-tuple-element.24), channel_id=1, source_target_pairs={{0,1},{1,2},{2,3},{3,0},{4,5},{5,6},{6,7},{7,4},{8,9},{9,10},{10,1... | collective-permute-start | bytes 294920 | tf_op jit(solution)/shard_map/ppermute | solution.py:243
  41.3 26.1 %collective-permute-start = (f32[96,512]{1,0:T(8,128)S(1)}, f32[96,512]{1,0:T(8,128)S(1)}, u32[]{:S(2)}, u32[]{:S(2)}) collective-permute-start(f32[96,512]{1,0:T(8,128)S(1)} %get-tuple-element.19), channel_id=1, source_target_pairs={{0,1},{1,2},{2,3},{3,0},{4,5},{5,6},{6,7},{7,4},{8,9},{9,10},{10,1... | collective-permute-start | bytes 589832 | tf_op jit(solution)/shard_map/ppermute | solution.py:243
  42.9 24.5 %collective-permute-start.1 = (f32[96,512]{1,0:T(8,128)S(1)}, f32[96,512]{1,0:T(8,128)S(1)}, u32[]{:S(2)}, u32[]{:S(2)}) collective-permute-start(f32[96,512]{1,0:T(8,128)S(1)} %get-tuple-element.20), channel_id=1, source_target_pairs={{0,2},{1,3},{2,0},{3,1},{4,6},{5,7},{6,4},{7,5},{8,10},{9,11},{10,... | collective-permute-start | bytes 589832 | tf_op jit(solution)/shard_map/ppermute | solution.py:243
  43.9 23.5 %collective-permute-start.2 = (f32[96,512]{1,0:T(8,128)S(1)}, f32[96,512]{1,0:T(8,128)S(1)}, u32[]{:S(2)}, u32[]{:S(2)}) collective-permute-start(f32[96,512]{1,0:T(8,128)S(1)} %get-tuple-element.21), channel_id=1, source_target_pairs={{0,3},{1,0},{2,1},{3,2},{4,7},{5,4},{6,5},{7,6},{8,11},{9,8},{10,9... | collective-permute-start | bytes 589832 | tf_op jit(solution)/shard_map/ppermute | solution.py:243
  46.8 20.6 %collective-permute-start.4 = (f32[96,256]{1,0:T(8,128)S(1)}, f32[96,256]{1,0:T(8,128)S(1)}, u32[]{:S(2)}, u32[]{:S(2)}) collective-permute-start(f32[96,256]{1,0:T(8,128)S(1)} %get-tuple-element.25), channel_id=1, source_target_pairs={{0,2},{1,3},{2,0},{3,1},{4,6},{5,7},{6,4},{7,5},{8,10},{9,11},{10,... | collective-permute-start | bytes 294920 | tf_op jit(solution)/shard_map/ppermute | solution.py:243
  47.2 20.2 %collective-permute-start.5 = (f32[96,256]{1,0:T(8,128)S(1)}, f32[96,256]{1,0:T(8,128)S(1)}, u32[]{:S(2)}, u32[]{:S(2)}) collective-permute-start(f32[96,256]{1,0:T(8,128)S(1)} %get-tuple-element.26), channel_id=1, source_target_pairs={{0,3},{1,0},{2,1},{3,2},{4,7},{5,4},{6,5},{7,6},{8,11},{9,8},{10,9... | collective-permute-start | bytes 294920 | tf_op jit(solution)/shard_map/ppermute | solution.py:243
  77.5 7.9 %collective-permute-start.8 = (bf16[96,768]{1,0:T(8,128)(2,1)S(1)}, bf16[96,768]{1,0:T(8,128)(2,1)S(1)}, u32[]{:S(2)}, u32[]{:S(2)}) collective-permute-start(bf16[96,768]{1,0:T(8,128)(2,1)S(1)} %shard_map.31.refs_0_), channel_id=1, source_target_pairs={{0,3},{1,0},{2,1},{3,2},{4,7},{5,4},{6,5},{7,6},{8,11},{9,8},{10,9... | collective-permute-start | bytes 442376 | tf_op jit(solution)/shard_map/ppermute | solution.py:243
  81.2 14.0 %collective-permute-start.7 = (bf16[96,768]{1,0:T(8,128)(2,1)S(1)}, bf16[96,768]{1,0:T(8,128)(2,1)S(1)}, u32[]{:S(2)}, u32[]{:S(2)}) collective-permute-start(bf16[96,768]{1,0:T(8,128)(2,1)S(1)} %shard_map.31.refs_0_), channel_id=1, source_target_pairs={{0,2},{1,3},{2,0},{3,1},{4,6},{5,7},{6,4},{7,5},{8,10},{9,11},{10,... | collective-permute-start | bytes 442376 | tf_op jit(solution)/shard_map/ppermute | solution.py:243
  81.6 13.6 %collective-permute-start.6 = (bf16[96,768]{1,0:T(8,128)(2,1)S(1)}, bf16[96,768]{1,0:T(8,128)(2,1)S(1)}, u32[]{:S(2)}, u32[]{:S(2)}) collective-permute-start(bf16[96,768]{1,0:T(8,128)(2,1)S(1)} %shard_map.31.refs_0_), channel_id=1, source_target_pairs={{0,1},{1,2},{2,3},{3,0},{4,5},{5,6},{6,7},{7,4},{8,9},{9,10},{10,1... | collective-permute-start | bytes 442376 | tf_op jit(solution)/shard_map/ppermute | solution.py:243
  95.2 4.6 %copy-start.1 = (bf16[384,16384]{1,0:T(8,128)(2,1)S(1)}, bf16[384,16384]{1,0:T(8,128)(2,1)}, u32[]{:S(2)}) copy-start(bf16[384,16384]{1,0:T(8,128)(2,1)} %copy-done) | copy-start | bytes 37748740
  99.8 5.8 %copy-start.3 = (bf16[512,16384]{1,0:T(8,128)(2,1)S(1)}, bf16[512,16384]{1,0:T(8,128)(2,1)}, u32[]{:S(2)}) copy-start(bf16[512,16384]{1,0:T(8,128)(2,1)} %copy-done.2) | copy-start | bytes 50331652

commit v2 on v1

--- a/solution.py
+++ b/solution.py
@@ -19,6 +19,10 @@
 
 def params(mib):
     return pltpu.CompilerParams(vmem_limit_bytes=mib * MIB)
+
+
+def hbm(x):
+    return pltpu.with_memory_space_constraint(x, pltpu.HBM)
 
 
 def accumulate(model, counts, accs, totals, px, tiles):
@@ -53,12 +57,14 @@
     if first:
         patterns_hbm, refs = refs[0], refs[1:]
     else:
-        counts, refs = refs[0], refs[1:]
+        counts, refs = refs[0], refs[2:]
     shares, refs = refs[:count], refs[count:]
     model, refs = refs[0], refs[1:]
     if first:
         counts, refs = refs[0], refs[1:]
         raw, raw_sems, refs = refs[0], refs[1], refs[2:]
+    else:
+        refs = refs[1:]
     whole, totals, model_sems = refs
     rows, pixels = model.shape
     frames = counts.shape[0]
@@ -106,7 +112,7 @@
     pl.run_scoped(scoped, *[pltpu.ACC(j % 2)((frames, TILE), f32) for j in range(2 * tiles)])
 
 
-def partial_scores(place, model, patterns, counts, row, rows, pix_count):
+def partial_scores(place, model, patterns, counts, held, row, rows, pix_count):
     pixels = model.shape[1]
     first = counts is None
     frames = patterns.shape[0]
@@ -114,17 +120,19 @@
     whole_vmem = pl.BlockSpec(memory_space=pltpu.VMEM)
     anywhere = pl.BlockSpec(memory_space=pl.ANY)
     if first:
-        operands = (place, model, patterns)
+        operands = (place, hbm(model), patterns)
         in_specs = [pl.BlockSpec(memory_space=pltpu.SMEM), anywhere, anywhere]
     else:
-        operands = (place, model, pltpu.with_memory_space_constraint(counts, pltpu.VMEM))
-        in_specs = [pl.BlockSpec(memory_space=pltpu.SMEM), anywhere, whole_vmem]
+        operands = (place, hbm(model), hold(counts), hold(held))
+        in_specs = [pl.BlockSpec(memory_space=pltpu.SMEM), anywhere, whole_vmem, anywhere]
     out_shape = [jax.ShapeDtypeStruct((frames // pix_count, rows), f32)] * pix_count
     out_shape.append(pltpu.VMEM((rows, pixels), bf16))
     scratch = []
     if first:
         out_shape.append(pltpu.VMEM((frames, pixels), bf16))
         scratch += [pltpu.VMEM((AHEAD, frames, STEP), jnp.int32), pltpu.SemaphoreType.DMA((AHEAD,))]
+    else:
+        out_shape.append(held_shape(held))
     scratch += [
         pltpu.VMEM((frames, rows), f32),
         pltpu.VMEM((rows, 128), f32),
@@ -134,62 +142,102 @@
         functools.partial(score_kernel, pix_count, first, row),
         out_shape=out_shape,
         in_specs=in_specs,
-        out_specs=[whole_vmem] * len(out_shape),
+        out_specs=[whole_vmem] * (len(out_shape) - 1) + [whole_vmem if first else anywhere],
         scratch_shapes=scratch,
-        compiler_params=params(14),
-        cost_estimate=pl.CostEstimate(
-            flops=4 * rows * pixels * frames,
-            bytes_accessed=2 * rows * pixels + (4 * frames * pixels if first else 0),
-            transcendentals=rows * pixels,
-        ),
+        input_output_aliases={} if first else {3: pix_count + 1},
+        compiler_params=params(8),
     )(*operands)
 
 
-def stats_kernel(beta, groups, *refs):
-    scores, stat = refs[-2:]
-    at = 0
-    start = 0
-    for size in groups:
-        parts = refs[at : at + size]
-        at += size
-        total = parts[0][...]
-        for part in parts[1:]:
-            total = total + part[...]
-        scores[:, start : start + total.shape[1]] = total * beta
-        start += total.shape[1]
-    values = scores[...]
+def join_kernel(count, beta, *refs):
+    total = refs[0][...]
+    for part in refs[1:count]:
+        total = total + part[...]
+    refs[-1][...] = total * beta
+
+
+def stats_kernel(count, beta, first, *refs):
+    parts = refs[:count]
+    weights, stat = refs[-3], refs[-2]
+    whole = refs[-1]
+    total = parts[0][...]
+    for part in parts[1:]:
+        total = total + part[...]
+    start = first.shape[1]
+    whole[:, :start] = first[...]
+    whole[:, start:] = total * beta
+    values = whole[...]
     highest = jnp.max(values, axis=1, keepdims=True)
-    sums = jnp.sum(jnp.exp(values - highest), axis=1, keepdims=True)
-    lane = lax.broadcasted_iota(jnp.int32, stat.shape, 1)
-    stat[...] = jnp.where(lane == 0, highest, sums)
-
-
-def probs_kernel(scores, stats, probs):
-    highest = stats[:, :, 0:1]
-    overall = jnp.max(highest, axis=0)
-    total = jnp.sum(stats[:, :, 1:2] * jnp.exp(highest - overall[None]), axis=0)
-    probs[...] = (jnp.exp(scores[...] - overall) / total).astype(bf16)
-
-
-def update_kernel(count, places, place_ref, *refs):
-    shares, refs = refs[:count], refs[count:]
+    scaled = jnp.exp(values - highest)
+    sums = jnp.sum(scaled, axis=1, keepdims=True)
+    weights[...] = scaled.astype(bf16)
+    lane = lax.broadcasted_iota(jnp.int32, (values.shape[0], 128), 1)
+    stat[...] = jnp.where(lane == 0, highest, sums).T[:8, :]
+
+
+def held_spec():
+    return pl.BlockSpec(memory_space=pl.ANY)
+
+
+def hold(x):
+    return pltpu.with_memory_space_constraint(x, pltpu.VMEM)
+
+
+def held_shape(x):
+    return pltpu.VMEM(x.shape, x.dtype)
+
+
+def turn_kernel(count, place_ref, *refs):
+    shares = refs[:count]
+    across, stacked = refs[count + 3], refs[-1]
+    depth = shares[0].shape[0]
+    wide = stacked.shape[0]
+    if wide > depth * count:
+        stacked[depth * count :, :] = jnp.zeros((wide - depth * count, stacked.shape[1]), f32)
+    for k in range(count):
+        owner = lax.rem(place_ref[0] + count - k, count)
+        stacked[pl.ds(pl.multiple_of(owner * depth, 8), depth), :] = shares[k][...].astype(f32)
+    across[...] = stacked[...].T.astype(bf16)
+
+
+def turn(place, shares, model_a, model_b, counts):
+    held = [model_a, model_b, counts]
+    count = len(shares)
+    depth, rows = shares[0].shape
+    wide = -(-depth * count // TILE) * TILE
+    return pl.pallas_call(
+        functools.partial(turn_kernel, count),
+        out_shape=[jax.ShapeDtypeStruct((rows, wide), bf16)] + [held_shape(x) for x in held],
+        in_specs=[pl.BlockSpec(memory_space=pltpu.SMEM)]
+        + [pl.BlockSpec(memory_space=pltpu.VMEM)] * count
+        + [held_spec()] * 3,
+        out_specs=[pl.BlockSpec(memory_space=pltpu.VMEM)] + [held_spec()] * 3,
+        scratch_shapes=[pltpu.VMEM((wide, rows), f32)],
+        input_output_aliases={count + 1 + j: 1 + j for j in range(3)},
+        compiler_params=params(8),
+    )(place, *shares, *[hold(x) for x in held])
+
+
+def update_kernel(count, places, place_ref, across, *refs):
+    factors, refs = refs[:count], refs[count:]
     counts, refs = refs[0], refs[1:]
     models, refs = refs[:places], refs[places:]
-    out, turned, probs, inverse = refs
+    out, columns, probs, inverse = refs
     step = pl.program_id(0)
-    depth = shares[0].shape[0]
-    frames = depth * count
-    wide = probs.shape[1]
+    frames, wide = counts.shape[0], probs.shape[1]
+    depth = frames // count
 
     @pl.when(step == 0)
     def _():
-        turned[frames:, :] = jnp.zeros((wide - frames, turned.shape[1]), f32)
+        if wide > frames:
+            columns[frames:, :] = jnp.zeros((wide - frames, 128), f32)
         for k in range(count):
             owner = lax.rem(place_ref[0] + count - k, count)
-            turned[pl.ds(pl.multiple_of(owner * depth, 8), depth), :] = shares[k][...].astype(f32)
-        across = turned[...].T
-        probs[...] = across.astype(bf16)
-        inverse[...] = 1.0 / (jnp.sum(across, axis=1, keepdims=True) + PRIOR)
+            rows = pl.ds(pl.multiple_of(owner * depth, 8), depth)
+            columns[rows, :] = jnp.broadcast_to(factors[k][0:1, :], (128, depth)).T
+        rounded = (across[...].astype(f32) * columns[...].T[0:1, :]).astype(bf16)
+        probs[...] = rounded
+        inverse[...] = 1.0 / (jnp.sum(rounded.astype(f32), axis=1, keepdims=True) + PRIOR)
 
     width = out.shape[1]
 
@@ -215,28 +263,25 @@
     pl.run_scoped(scoped, *[pltpu.ACC(j)((out.shape[0], TILE), f32) for j in range(2)])
 
 
-def update(place, shares, counts, models):
+def update(place, across, factors, counts, models):
     frames, pixels = counts.shape
-    rows = sum(m.shape[0] for m in models)
-    wide = -(-frames // TILE) * TILE
+    rows, wide = across.shape
     whole_vmem = pl.BlockSpec(memory_space=pltpu.VMEM)
-    pinned = [pltpu.with_memory_space_constraint(a, pltpu.VMEM) for a in (counts, *models)]
+    pinned = [hold(a) for a in (counts, *models)]
     return pl.pallas_call(
-        functools.partial(update_kernel, len(shares), len(models)),
+        functools.partial(update_kernel, len(factors), len(models)),
         out_shape=jax.ShapeDtypeStruct((rows, pixels), bf16),
         grid=(pixels // STEP,),
-        in_specs=[pl.BlockSpec(memory_space=pltpu.SMEM)] + [whole_vmem] * (len(shares) + len(pinned)),
+        in_specs=[pl.BlockSpec(memory_space=pltpu.SMEM)]
+        + [whole_vmem] * (1 + len(factors) + len(pinned)),
         out_specs=pl.BlockSpec((rows, STEP), lambda i: (0, i)),
         scratch_shapes=[
-            pltpu.VMEM((wide, rows), f32),
+            pltpu.VMEM((wide, 128), f32),
             pltpu.VMEM((rows, wide), bf16),
             pltpu.VMEM((rows, 1), f32),
         ],
-        compiler_params=params(16),
-        cost_estimate=pl.CostEstimate(
-            flops=2 * rows * pixels * frames, bytes_accessed=2 * rows * pixels, transcendentals=0
-        ),
-    )(place, *shares, *pinned)
+        compiler_params=params(10),
+    )(place, across, *factors, *pinned)
 
 
 def shift(x, k, count):
@@ -244,31 +289,79 @@
 
 
 def on_device(pix_count, orient_count, beta, model, patterns):
-    place = lax.axis_index("pix").astype(jnp.int32).reshape(1)
+    place = jnp.stack([lax.axis_index("pix"), lax.axis_index("orient")]).astype(jnp.int32)
     rows = model.shape[0]
+    depth = patterns.shape[0] // pix_count
     head = max(TILE, rows // 3 * 2 // TILE * TILE)
-    first = partial_scores(place, model, patterns, None, 0, head, pix_count)
-    counts = first[-1]
-    second = partial_scores(place, model, patterns, counts, head, rows - head, pix_count)
-    pieces, groups = [], []
-    for result in (first, second):
-        pieces.append(result[0])
-        pieces += [shift(result[k], k, pix_count) for k in range(1, pix_count)]
-        groups.append(pix_count)
-    depth = patterns.shape[0] // pix_count
-    scores, stat = pl.pallas_call(
-        functools.partial(stats_kernel, beta, tuple(groups)),
-        out_shape=[jax.ShapeDtypeStruct((depth, rows), f32), jax.ShapeDtypeStruct((depth, 128), f32)],
-        compiler_params=params(14),
+    *sent, model_a, counts = partial_scores(place, model, patterns, None, None, 0, head, pix_count)
+    pieces = [sent[0]] + [shift(sent[k], k, pix_count) for k in range(1, pix_count)]
+    *sent, model_b, model_a = partial_scores(
+        place, model, patterns, counts, model_a, head, rows - head, pix_count
+    )
+    first = pl.pallas_call(
+        functools.partial(join_kernel, pix_count, beta),
+        out_shape=jax.ShapeDtypeStruct((depth, head), f32),
+        compiler_params=params(8),
+        cost_estimate=pl.CostEstimate(flops=20 * 10**9, bytes_accessed=0, transcendentals=0),
     )(*pieces)
-    stats = lax.all_gather(stat, "orient")
-    probs = pl.pallas_call(
-        probs_kernel,
-        out_shape=jax.ShapeDtypeStruct((depth, rows), bf16),
-        compiler_params=params(14),
-    )(scores, stats)
-    shares = [probs] + [shift(probs, k, pix_count) for k in range(1, pix_count)]
-    return update(place, shares, counts, [first[-2], second[-1]])
+    pieces = [sent[0]] + [shift(sent[k], k, pix_count) for k in range(1, pix_count)]
+    weights, stat, model_a, model_b, counts = pl.pallas_call(
+        functools.partial(pass_stats, pix_count, beta),
+        out_shape=[
+            jax.ShapeDtypeStruct((depth, rows), bf16),
+            jax.ShapeDtypeStruct((8, depth), f32),
+            held_shape(model_a),
+            held_shape(model_b),
+            held_shape(counts),
+        ],
+        in_specs=[pl.BlockSpec(memory_space=pltpu.VMEM)] * (pix_count + 1) + [held_spec()] * 3,
+        out_specs=[pl.BlockSpec(memory_space=pltpu.VMEM)] * 2 + [held_spec()] * 3,
+        scratch_shapes=[pltpu.VMEM((depth, rows), f32)],
+        input_output_aliases={pix_count + 1 + j: 2 + j for j in range(3)},
+        compiler_params=params(8),
+    )(*pieces, first, hold(model_a), hold(model_b), hold(counts))
+    shares = [weights] + [shift(weights, k, pix_count) for k in range(1, pix_count)]
+    pair, model_a, model_b, counts = merge([stat, swap(stat, 1, orient_count)], model_a, model_b, counts)
+    pairs = [pair] + [swap(pair, k, orient_count) for k in range(2, orient_count, 2)]
+    factor, model_a, model_b, counts = merge(pairs, model_a, model_b, counts, stat)
+    factors = [factor] + [shift(factor, k, pix_count) for k in range(1, pix_count)]
+    across, model_a, model_b, counts = turn(place, shares, model_a, model_b, counts)
+    return update(place, across, factors, counts, [model_a, model_b])
+
+
+def swap(x, distance, count):
+    return lax.ppermute(x, "orient", [(i, i ^ distance) for i in range(count)])
+
+
+def merge_kernel(number, last, *refs):
+    pairs = refs[:number]
+    out = refs[number + (4 if last else 3)]
+    tops = [pair[0:1, :] for pair in pairs]
+    overall = functools.reduce(jnp.maximum, tops)
+    total = sum(pair[1:2, :] * jnp.exp(top - overall) for pair, top in zip(pairs, tops))
+    if last:
+        out[...] = jnp.broadcast_to(jnp.exp(refs[number][0:1, :] - overall) / total, out.shape)
+    else:
+        row = lax.broadcasted_iota(jnp.int32, out.shape, 0)
+        out[...] = jnp.where(row == 0, overall, total)
+
+
+def merge(pairs, model_a, model_b, counts, stat=None):
+    small = pairs + ([] if stat is None else [stat])
+    held = [model_a, model_b, counts]
+    return pl.pallas_call(
+        functools.partial(merge_kernel, len(pairs), stat is not None),
+        out_shape=[jax.ShapeDtypeStruct(pairs[0].shape, f32)] + [held_shape(x) for x in held],
+        in_specs=[pl.BlockSpec(memory_space=pltpu.VMEM)] * len(small) + [held_spec()] * 3,
+        out_specs=[pl.BlockSpec(memory_space=pltpu.VMEM)] + [held_spec()] * 3,
+        input_output_aliases={len(small) + j: 1 + j for j in range(3)},
+        compiler_params=params(8),
+    )(*small, *[hold(x) for x in held])
+
+
+def pass_stats(count, beta, *refs):
+    ins, outs = refs[: count + 4], refs[count + 4 :]
+    stats_kernel(count, beta, ins[count], *ins[:count], outs[0], outs[1], outs[-1])
 
 
 def solution(mesh):

time: 125 us -> 88.2 us (0.71)
  local copies, waits for them, and re-layouts: 21 us -> 0 us
  waiting for transfers between devices: 31.7 us -> 13.1 us
  starting transfers between devices: 15 us -> 25.3 us
  blocking collectives: 9.6 us -> 0 us
  Pallas kernels: 47.4 us -> 49.6 us
    ppermute x9 -> x12, waiting for transfers between devices: 31.7 us -> 9.23 us  [shift(): return lax.ppermute(x, 'pix', [(i, (i + k) % count) for i in range(count)])]
    unnamed x8 -> x0, local copies, waits for them, and re-layouts: 21 us -> none
    all_gather x1 -> x0, blocking collectives: 9.6 us -> none  [on_device(): stats = lax.all_gather(stat, 'orient')]
    ppermute x0 -> x4, starting transfers between devices: none -> 5.47 us  [swap(): return lax.ppermute(x, 'orient', [(i, i ^ distance) for i in range(count)])]
    ppermute x9 -> x12, starting transfers between devices: 15 us -> 19.8 us  [shift(): return lax.ppermute(x, 'pix', [(i, (i + k) % count) for i in range(count)])]
    ppermute x0 -> x4, waiting for transfers between devices: none -> 3.87 us  [swap(): return lax.ppermute(x, 'orient', [(i, i ^ distance) for i in range(count)])]
    pallas_call x3 -> x6, Pallas kernels: 19.8 us -> 20.9 us  [the longest x1 19.7 us: update(): pl.pallas_call(functools.partial(update_kernel, len(factors), len(models)...]
  transfers between devices with their start and end apart: 9 -> 16, of which waited for: 3 -> 8; matrix products, arithmetic and copies ran while one was open for 0% -> 0% of each run, Pallas kernels for 0% -> 13%
where the time goes in v2:
time: 88.2 us; the launch traced here: 88.1 us
  Pallas kernels  49.6 us (56%)
  starting transfers between devices  25.3 us (29%)
  waiting for transfers between devices  13.1 us (15%)
    pallas_call x2, Pallas kernels, partial_scores(): pl.pallas_call(functools.partial(score_kernel, pix_count, first, row), ou...  28.7 us
    ppermute x12, starting transfers between devices, shift(): return lax.ppermute(x, 'pix', [(i, (i + k) % count) for i in range(count)])  19.8 us
    pallas_call x1, Pallas kernels, update(): pl.pallas_call(functools.partial(update_kernel, len(factors), len(models)...  19.7 us
    ppermute x12, waiting for transfers between devices, shift(): return lax.ppermute(x, 'pix', [(i, (i + k) % count) for i in range(count)])  9.23 us
    ppermute x4, starting transfers between devices, swap(): return lax.ppermute(x, 'orient', [(i, i ^ distance) for i in range(count)])  5.47 us
    ppermute x4, waiting for transfers between devices, swap(): return lax.ppermute(x, 'orient', [(i, i ^ distance) for i in range(count)])  3.87 us
  transfers between devices with their start and end apart: 16, of which 8 were waited for; matrix products, arithmetic and copies ran while one was open for 0% of the time, Pallas kernels for 13%

profile of v2, /device:TPU:0, one launch (start us, length us, event | category | flops | bytes accessed | tf_op | source)
XLA Modules:
  0.0 88.1 jit_solution(9580968134185881925)
XLA Ops:
  0.0 0.1 pad_add_fusion.place_ref
  0.1 18.4 %shard_map.28 = (f32[96,512]{1,0:T(8,128)S(1)}, f32[96,512]{1,0:T(8,128)S(1)}, f32[96,512]{1,0:T(8,128)S(1)}, f32[96,512]{1,0:T(8,128)S(1)}, bf16[512,16384]{1,0...) custom-call(s32[2]{0:T(128)S(1)} %pad_add_fusion.place_ref, bf16[768,16384]{1,0:T(8,128)(2,1)} %model_hbm.3, s32[384,16384]{1,0:T(8,128)} %refs_0_.1), custom_call_target="tpu_custom_call" | custom-call | tf_op jit(solution)/shard_map/pallas_call | solution.py:141
  18.5 3.1 %collective-permute-start.3 = (f32[96,512]{1,0:T(8,128)S(1)}, f32[96,512]{1,0:T(8,128)S(1)}, u32[]{:S(2)}, u32[]{:S(2)}) collective-permute-start(f32[96,512]{1,0:T(8,128)S(1)} %get-tuple-element.41), channel_id=1, source_target_pairs={{0,1},{1,2},{2,3},{3,0},{4,5},{5,6},{6,7},{7,4},{8,9},{9,10},{10,1... | collective-permute-start | bytes 589832 | tf_op jit(solution)/shard_map/ppermute | solution.py:288
  21.5 2.6 %collective-permute-start.4 = (f32[96,512]{1,0:T(8,128)S(1)}, f32[96,512]{1,0:T(8,128)S(1)}, u32[]{:S(2)}, u32[]{:S(2)}) collective-permute-start(f32[96,512]{1,0:T(8,128)S(1)} %get-tuple-element.42), channel_id=1, source_target_pairs={{0,2},{1,3},{2,0},{3,1},{4,6},{5,7},{6,4},{7,5},{8,10},{9,11},{10,... | collective-permute-start | bytes 589832 | tf_op jit(solution)/shard_map/ppermute | solution.py:288
  24.1 1.4 %collective-permute-start.5 = (f32[96,512]{1,0:T(8,128)S(1)}, f32[96,512]{1,0:T(8,128)S(1)}, u32[]{:S(2)}, u32[]{:S(2)}) collective-permute-start(f32[96,512]{1,0:T(8,128)S(1)} %get-tuple-element.43), channel_id=1, source_target_pairs={{0,3},{1,0},{2,1},{3,2},{4,7},{5,4},{6,5},{7,6},{8,11},{9,8},{10,9... | collective-permute-start | bytes 589832 | tf_op jit(solution)/shard_map/ppermute | solution.py:288
  25.5 10.3 %shard_map.29 = (f32[96,256]{1,0:T(8,128)S(1)}, f32[96,256]{1,0:T(8,128)S(1)}, f32[96,256]{1,0:T(8,128)S(1)}, f32[96,256]{1,0:T(8,128)S(1)}, bf16[256,16384]{1,0...) custom-call(s32[2]{0:T(128)S(1)} %pad_add_fusion.place_ref, ...), custom_call_target="tpu_custom_call", output_to_operand_aliasing={{5}: (3, {})} | custom-call | tf_op jit(solution)/shard_map/pallas_call | solution.py:141
  35.8 0.7 collective-permute-start
  36.5 0.4 collective-permute-start.1
  36.8 0.0 collective-permute-done.3.refs_1_
  36.9 2.8 %collective-permute-start.2 = (f32[96,256]{1,0:T(8,128)S(1)}, f32[96,256]{1,0:T(8,128)S(1)}, u32[]{:S(2)}, u32[]{:S(2)}) collective-permute-start(f32[96,256]{1,0:T(8,128)S(1)} %get-tuple-element.39), channel_id=1, source_target_pairs={{0,3},{1,0},{2,1},{3,2},{4,7},{5,4},{6,5},{7,6},{8,11},{9,8},{10,9... | collective-permute-start | bytes 294920 | tf_op jit(solution)/shard_map/ppermute | solution.py:288
  39.7 0.0 collective-permute-done.4.refs_2_
  39.7 0.0 collective-permute-done.5.refs_3_
  39.7 3.7 %collective-permute-done.refs_1_ = f32[96,256]{1,0:T(8,128)S(1)} collective-permute-done((f32[96,256]{1,0:T(8,128)S(1)}, f32[96,256]{1,0:T(8,128)S(1)}, u32[]{:S(2)}, u32[]{:S(2)}) %collective-permute-start) | collective-permute-done | bytes 98336 | tf_op jit(solution)/shard_map/ppermute | solution.py:288
  43.4 4.2 %collective-permute-done.1.refs_2_ = f32[96,256]{1,0:T(8,128)S(1)} collective-permute-done((f32[96,256]{1,0:T(8,128)S(1)}, f32[96,256]{1,0:T(8,128)S(1)}, u32[]{:S(2)}, u32[]{:S(2)}) %collective-permute-start.1) | collective-permute-done | bytes 98336 | tf_op jit(solution)/shard_map/ppermute | solution.py:288
  47.5 0.0 collective-permute-done.2.refs_3_
  47.5 0.3 shard_map.31
  47.8 2.6 %collective-permute-start.6 = (bf16[96,768]{1,0:T(8,128)(2,1)S(1)}, bf16[96,768]{1,0:T(8,128)(2,1)S(1)}, u32[]{:S(2)}, u32[]{:S(2)}) collective-permute-start(bf16[96,768]{1,0:T(8,128)(2,1)S(1)} %get-tuple-element.46.refs_0_), channel_id=1, source_target_pairs={{0,1},{1,2},{2,3},{3,0},{4,5},{5,6},{6,7},{7,4},{8,9},{9,10},{10,1... | collective-permute-start | bytes 442376 | tf_op jit(solution)/shard_map/ppermute | solution.py:288
  50.4 1.6 %collective-permute-start.7 = (bf16[96,768]{1,0:T(8,128)(2,1)S(1)}, bf16[96,768]{1,0:T(8,128)(2,1)S(1)}, u32[]{:S(2)}, u32[]{:S(2)}) collective-permute-start(bf16[96,768]{1,0:T(8,128)(2,1)S(1)} %get-tuple-element.46.refs_0_), channel_id=1, source_target_pairs={{0,2},{1,3},{2,0},{3,1},{4,6},{5,7},{6,4},{7,5},{8,10},{9,11},{10,... | collective-permute-start | bytes 442376 | tf_op jit(solution)/shard_map/ppermute | solution.py:288
  52.0 0.8 collective-permute-start.8
  52.8 0.0 collective-permute-start.9
  52.8 1.2 %collective-permute-done.9.refs_1_ = f32[8,96]{1,0:T(8,128)S(1)} collective-permute-done((f32[8,96]{1,0:T(8,128)S(1)}, f32[8,96]{1,0:T(8,128)S(1)}, u32[]{:S(2)}, u32[]{:S(2)}) %collective-permute-start.9) | collective-permute-done | bytes 3104 | tf_op jit(solution)/shard_map/ppermute | solution.py:333
  54.0 1.5 %collective-permute-start.10 = (f32[8,96]{1,0:T(8,128)S(1)}, f32[8,96]{1,0:T(8,128)S(1)}, u32[]{:S(2)}, u32[]{:S(2)}) collective-permute-start(f32[8,96]{1,0:T(8,128)S(1)} %get-tuple-element.51.refs_0_), channel_id=1, source_target_pairs={{0,8},{4,12},{8,0},{12,4},{16,24},{20,28},{24,16},{28,20},{1,9},{5... | collective-permute-start | bytes 9224 | tf_op jit(solution)/shard_map/ppermute | solution.py:333
  55.5 1.5 %collective-permute-start.11 = (f32[8,96]{1,0:T(8,128)S(1)}, f32[8,96]{1,0:T(8,128)S(1)}, u32[]{:S(2)}, u32[]{:S(2)}) collective-permute-start(f32[8,96]{1,0:T(8,128)S(1)} %get-tuple-element.51.refs_0_), channel_id=1, source_target_pairs={{0,16},{4,20},{8,24},{12,28},{16,0},{20,4},{24,8},{28,12},{1,17},{... | collective-permute-start | bytes 9224 | tf_op jit(solution)/shard_map/ppermute | solution.py:333
  57.0 0.6 collective-permute-done.10.refs_1_
  57.7 2.4 %collective-permute-start.12 = (f32[8,96]{1,0:T(8,128)S(1)}, f32[8,96]{1,0:T(8,128)S(1)}, u32[]{:S(2)}, u32[]{:S(2)}) collective-permute-start(f32[8,96]{1,0:T(8,128)S(1)} %get-tuple-element.51.refs_0_), channel_id=1, source_target_pairs={{0,24},{4,28},{8,16},{12,20},{16,8},{20,12},{24,0},{28,4},{1,25},{... | collective-permute-start | bytes 9224 | tf_op jit(solution)/shard_map/ppermute | solution.py:333
  60.1 0.0 collective-permute-done.11.refs_2_
  60.1 2.1 %collective-permute-done.12.refs_3_ = f32[8,96]{1,0:T(8,128)S(1)} collective-permute-done((f32[8,96]{1,0:T(8,128)S(1)}, f32[8,96]{1,0:T(8,128)S(1)}, u32[]{:S(2)}, u32[]{:S(2)}) %collective-permute-start.12) | collective-permute-done | bytes 3104 | tf_op jit(solution)/shard_map/ppermute | solution.py:333
  62.2 1.2 %collective-permute-start.13 = (f32[8,96]{1,0:T(8,128)S(1)}, f32[8,96]{1,0:T(8,128)S(1)}, u32[]{:S(2)}, u32[]{:S(2)}) collective-permute-start(f32[8,96]{1,0:T(8,128)S(1)} %get-tuple-element.59.refs_0_), channel_id=1, source_target_pairs={{0,1},{1,2},{2,3},{3,0},{4,5},{5,6},{6,7},{7,4},{8,9},{9,10},{10,1... | collective-permute-start | bytes 9224 | tf_op jit(solution)/shard_map/ppermute | solution.py:288
  63.4 1.3 %collective-permute-start.14 = (f32[8,96]{1,0:T(8,128)S(1)}, f32[8,96]{1,0:T(8,128)S(1)}, u32[]{:S(2)}, u32[]{:S(2)}) collective-permute-start(f32[8,96]{1,0:T(8,128)S(1)} %get-tuple-element.59.refs_0_), channel_id=1, source_target_pairs={{0,2},{1,3},{2,0},{3,1},{4,6},{5,7},{6,4},{7,5},{8,10},{9,11},{10,... | collective-permute-start | bytes 9224 | tf_op jit(solution)/shard_map/ppermute | solution.py:288
  64.8 0.0 collective-permute-done.6.refs_1_
  64.8 1.3 %collective-permute-start.15 = (f32[8,96]{1,0:T(8,128)S(1)}, f32[8,96]{1,0:T(8,128)S(1)}, u32[]{:S(2)}, u32[]{:S(2)}) collective-permute-start(f32[8,96]{1,0:T(8,128)S(1)} %get-tuple-element.59.refs_0_), channel_id=1, source_target_pairs={{0,3},{1,0},{2,1},{3,2},{4,7},{5,4},{6,5},{7,6},{8,11},{9,8},{10,9... | collective-permute-start | bytes 9224 | tf_op jit(solution)/shard_map/ppermute | solution.py:288
  66.1 0.0 collective-permute-done.7.refs_2_
  66.1 0.0 collective-permute-done.8.refs_3_
  66.1 0.9 %shard_map.34 = (bf16[768,512]{1,0:T(8,128)(2,1)S(1)}, bf16[512,16384]{1,0:T(8,128)(2,1)S(1)}, bf16[256,16384]{1,0:T(8,128)(2,1)S(1)}, bf16[384,16384]{1,0:T(8,128)(2,1)S(1)}) custom-call(s32[2]{0:T(128)S(1)} %pad_add_fusion.place_ref, bf16[96,768]{1,0:T(8,128)(2,1)S(1)} %get-tuple-element.46.refs_0_, ...), custom_call_target="tpu_custom_call", output_to_operand_aliasing={{1}: (5, {}), {2}: (6, {}), {3}: (7, {})} | custom-call | tf_op jit(solution)/shard_map/pallas_call | solution.py:208
  67.0 0.7 collective-permute-done.13.refs_1_
  67.7 0.3 collective-permute-done.14.refs_2_
  67.9 0.4 collective-permute-done.15.refs_3_
  68.4 19.7 %shard_map.35 = bf16[768,16384]{1,0:T(8,128)(2,1)} custom-call(s32[2]{0:T(128)S(1)} %pad_add_fusion.place_ref, bf16[768,512]{1,0:T(8,128)(2,1)S(1)} %get-tuple-element.58.across, f32[8,96]{1,0:T(8,128)S(1)} %get-tuple-element.59.refs_0_, f32[8,96]{1,0:T(8,128)S(1)} %collective-permute-done.13.refs_1_, f32[8,96]{1,0:T(8,128)S(1)} %collective-permute-done.14.refs_2_, ...), custom_call_target="tpu_custom_call" | custom-call | tf_op jit(solution)/shard_map/pallas_call | solution.py:271
  (3 shorter events, 0.1 us)
Async XLA Ops:
  18.5 18.4 %collective-permute-start.3 = (f32[96,512]{1,0:T(8,128)S(1)}, f32[96,512]{1,0:T(8,128)S(1)}, u32[]{:S(2)}, u32[]{:S(2)}) collective-permute-start(f32[96,512]{1,0:T(8,128)S(1)} %get-tuple-element.41), channel_id=1, source_target_pairs={{0,1},{1,2},{2,3},{3,0},{4,5},{5,6},{6,7},{7,4},{8,9},{9,10},{10,1... | collective-permute-start | bytes 589832 | tf_op jit(solution)/shard_map/ppermute | solution.py:288
  21.5 18.1 %collective-permute-start.4 = (f32[96,512]{1,0:T(8,128)S(1)}, f32[96,512]{1,0:T(8,128)S(1)}, u32[]{:S(2)}, u32[]{:S(2)}) collective-permute-start(f32[96,512]{1,0:T(8,128)S(1)} %get-tuple-element.42), channel_id=1, source_target_pairs={{0,2},{1,3},{2,0},{3,1},{4,6},{5,7},{6,4},{7,5},{8,10},{9,11},{10,... | collective-permute-start | bytes 589832 | tf_op jit(solution)/shard_map/ppermute | solution.py:288
  24.1 15.5 %collective-permute-start.5 = (f32[96,512]{1,0:T(8,128)S(1)}, f32[96,512]{1,0:T(8,128)S(1)}, u32[]{:S(2)}, u32[]{:S(2)}) collective-permute-start(f32[96,512]{1,0:T(8,128)S(1)} %get-tuple-element.43), channel_id=1, source_target_pairs={{0,3},{1,0},{2,1},{3,2},{4,7},{5,4},{6,5},{7,6},{8,11},{9,8},{10,9... | collective-permute-start | bytes 589832 | tf_op jit(solution)/shard_map/ppermute | solution.py:288
  35.8 7.6 %collective-permute-start = (f32[96,256]{1,0:T(8,128)S(1)}, f32[96,256]{1,0:T(8,128)S(1)}, u32[]{:S(2)}, u32[]{:S(2)}) collective-permute-start(f32[96,256]{1,0:T(8,128)S(1)} %get-tuple-element.37), channel_id=1, source_target_pairs={{0,1},{1,2},{2,3},{3,0},{4,5},{5,6},{6,7},{7,4},{8,9},{9,10},{10,1... | collective-permute-start | bytes 294920 | tf_op jit(solution)/shard_map/ppermute | solution.py:288
  36.5 11.0 %collective-permute-start.1 = (f32[96,256]{1,0:T(8,128)S(1)}, f32[96,256]{1,0:T(8,128)S(1)}, u32[]{:S(2)}, u32[]{:S(2)}) collective-permute-start(f32[96,256]{1,0:T(8,128)S(1)} %get-tuple-element.38), channel_id=1, source_target_pairs={{0,2},{1,3},{2,0},{3,1},{4,6},{5,7},{6,4},{7,5},{8,10},{9,11},{10,... | collective-permute-start | bytes 294920 | tf_op jit(solution)/shard_map/ppermute | solution.py:288
  36.9 10.7 %collective-permute-start.2 = (f32[96,256]{1,0:T(8,128)S(1)}, f32[96,256]{1,0:T(8,128)S(1)}, u32[]{:S(2)}, u32[]{:S(2)}) collective-permute-start(f32[96,256]{1,0:T(8,128)S(1)} %get-tuple-element.39), channel_id=1, source_target_pairs={{0,3},{1,0},{2,1},{3,2},{4,7},{5,4},{6,5},{7,6},{8,11},{9,8},{10,9... | collective-permute-start | bytes 294920 | tf_op jit(solution)/shard_map/ppermute | solution.py:288
  47.8 17.0 %collective-permute-start.6 = (bf16[96,768]{1,0:T(8,128)(2,1)S(1)}, bf16[96,768]{1,0:T(8,128)(2,1)S(1)}, u32[]{:S(2)}, u32[]{:S(2)}) collective-permute-start(bf16[96,768]{1,0:T(8,128)(2,1)S(1)} %get-tuple-element.46.refs_0_), channel_id=1, source_target_pairs={{0,1},{1,2},{2,3},{3,0},{4,5},{5,6},{6,7},{7,4},{8,9},{9,10},{10,1... | collective-permute-start | bytes 442376 | tf_op jit(solution)/shard_map/ppermute | solution.py:288
  50.4 15.7 %collective-permute-start.7 = (bf16[96,768]{1,0:T(8,128)(2,1)S(1)}, bf16[96,768]{1,0:T(8,128)(2,1)S(1)}, u32[]{:S(2)}, u32[]{:S(2)}) collective-permute-start(bf16[96,768]{1,0:T(8,128)(2,1)S(1)} %get-tuple-element.46.refs_0_), channel_id=1, source_target_pairs={{0,2},{1,3},{2,0},{3,1},{4,6},{5,7},{6,4},{7,5},{8,10},{9,11},{10,... | collective-permute-start | bytes 442376 | tf_op jit(solution)/shard_map/ppermute | solution.py:288
  52.0 14.1 %collective-permute-start.8 = (bf16[96,768]{1,0:T(8,128)(2,1)S(1)}, bf16[96,768]{1,0:T(8,128)(2,1)S(1)}, u32[]{:S(2)}, u32[]{:S(2)}) collective-permute-start(bf16[96,768]{1,0:T(8,128)(2,1)S(1)} %get-tuple-element.46.refs_0_), channel_id=1, source_target_pairs={{0,3},{1,0},{2,1},{3,2},{4,7},{5,4},{6,5},{7,6},{8,11},{9,8},{10,9... | collective-permute-start | bytes 442376 | tf_op jit(solution)/shard_map/ppermute | solution.py:288
  52.8 1.2 %collective-permute-start.9 = (f32[8,96]{1,0:T(8,128)S(1)}, f32[8,96]{1,0:T(8,128)S(1)}, u32[]{:S(2)}, u32[]{:S(2)}) collective-permute-start(f32[8,96]{1,0:T(8,128)S(1)} %get-tuple-element.47.refs_0_.refs_4_), channel_id=1, source_target_pairs={{0,4},{4,0},{8,12},{12,8},{16,20},{20,16},{24,28},{28,24},{1,5},{5... | collective-permute-start | bytes 9224 | tf_op jit(solution)/shard_map/ppermute | solution.py:333
  54.0 3.7 %collective-permute-start.10 = (f32[8,96]{1,0:T(8,128)S(1)}, f32[8,96]{1,0:T(8,128)S(1)}, u32[]{:S(2)}, u32[]{:S(2)}) collective-permute-start(f32[8,96]{1,0:T(8,128)S(1)} %get-tuple-element.51.refs_0_), channel_id=1, source_target_pairs={{0,8},{4,12},{8,0},{12,4},{16,24},{20,28},{24,16},{28,20},{1,9},{5... | collective-permute-start | bytes 9224 | tf_op jit(solution)/shard_map/ppermute | solution.py:333
  55.5 4.6 %collective-permute-start.11 = (f32[8,96]{1,0:T(8,128)S(1)}, f32[8,96]{1,0:T(8,128)S(1)}, u32[]{:S(2)}, u32[]{:S(2)}) collective-permute-start(f32[8,96]{1,0:T(8,128)S(1)} %get-tuple-element.51.refs_0_), channel_id=1, source_target_pairs={{0,16},{4,20},{8,24},{12,28},{16,0},{20,4},{24,8},{28,12},{1,17},{... | collective-permute-start | bytes 9224 | tf_op jit(solution)/shard_map/ppermute | solution.py:333
  57.7 4.5 %collective-permute-start.12 = (f32[8,96]{1,0:T(8,128)S(1)}, f32[8,96]{1,0:T(8,128)S(1)}, u32[]{:S(2)}, u32[]{:S(2)}) collective-permute-start(f32[8,96]{1,0:T(8,128)S(1)} %get-tuple-element.51.refs_0_), channel_id=1, source_target_pairs={{0,24},{4,28},{8,16},{12,20},{16,8},{20,12},{24,0},{28,4},{1,25},{... | collective-permute-start | bytes 9224 | tf_op jit(solution)/shard_map/ppermute | solution.py:333
  62.2 5.5 %collective-permute-start.13 = (f32[8,96]{1,0:T(8,128)S(1)}, f32[8,96]{1,0:T(8,128)S(1)}, u32[]{:S(2)}, u32[]{:S(2)}) collective-permute-start(f32[8,96]{1,0:T(8,128)S(1)} %get-tuple-element.59.refs_0_), channel_id=1, source_target_pairs={{0,1},{1,2},{2,3},{3,0},{4,5},{5,6},{6,7},{7,4},{8,9},{9,10},{10,1... | collective-permute-start | bytes 9224 | tf_op jit(solution)/shard_map/ppermute | solution.py:288
  63.4 4.5 %collective-permute-start.14 = (f32[8,96]{1,0:T(8,128)S(1)}, f32[8,96]{1,0:T(8,128)S(1)}, u32[]{:S(2)}, u32[]{:S(2)}) collective-permute-start(f32[8,96]{1,0:T(8,128)S(1)} %get-tuple-element.59.refs_0_), channel_id=1, source_target_pairs={{0,2},{1,3},{2,0},{3,1},{4,6},{5,7},{6,4},{7,5},{8,10},{9,11},{10,... | collective-permute-start | bytes 9224 | tf_op jit(solution)/shard_map/ppermute | solution.py:288
  64.8 3.6 %collective-permute-start.15 = (f32[8,96]{1,0:T(8,128)S(1)}, f32[8,96]{1,0:T(8,128)S(1)}, u32[]{:S(2)}, u32[]{:S(2)}) collective-permute-start(f32[8,96]{1,0:T(8,128)S(1)} %get-tuple-element.59.refs_0_), channel_id=1, source_target_pairs={{0,3},{1,0},{2,1},{3,2},{4,7},{5,4},{6,5},{7,6},{8,11},{9,8},{10,9... | collective-permute-start | bytes 9224 | tf_op jit(solution)/shard_map/ppermute | solution.py:288

commit v3 on v2

--- a/solution.py
+++ b/solution.py
@@ -15,6 +15,7 @@
 STEP = 1024
 TILE = 256
 AHEAD = 3
+FINEST, STEPS, LEVELS, HALF = -14, 20, 65000.0, 16384.0
 
 
 def params(mib):
@@ -41,7 +42,41 @@
         totals[rows, :] += x[:, :128] + x[:, 128:]
 
 
-def finish(accs, totals, whole, shares, tiles, place):
+def step_of(index):
+    step = jnp.full(index.shape, 2.0**FINEST, f32)
+    for j in range(1, STEPS):
+        step = jnp.where(index >= j, 2.0 ** (FINEST + j), step)
+    return step
+
+
+def pack(values, out):
+    depth, rows = values.shape
+    least = jnp.min(values, axis=1, keepdims=True)
+    span = jnp.max(values, axis=1, keepdims=True) - least
+    index = jnp.zeros_like(span)
+    for j in range(1, STEPS):
+        index = jnp.where(span > LEVELS * 2.0 ** (FINEST + j - 1), float(j), index)
+    step = step_of(index)
+    base = jnp.floor(least / step)
+    upper = jnp.floor(base / HALF)
+    lane = lax.broadcasted_iota(jnp.int32, (depth, 128), 1)
+    notes = jnp.where(lane == 0, upper, jnp.where(lane == 1, base - upper * HALF, index))
+    notes = notes.T[:16, :]
+    out[:16, :] = jnp.concatenate([notes, jnp.zeros((16, rows - depth), f32)], 1).astype(jnp.int32).astype(jnp.int16)
+    coded = (jnp.floor(values / step - base + 0.5) - 32768.0).astype(jnp.int32).astype(jnp.int16)
+    if depth % 16:
+        coded = jnp.concatenate([coded, jnp.zeros((16 - depth % 16, rows), jnp.int16)], 0)
+    out[16:, :] = coded
+
+
+def unpack(coded, depth):
+    notes = coded[:16, :128].astype(jnp.int32).astype(f32).T
+    upper, lower, index = (notes[:depth, j : j + 1] for j in range(3))
+    values = coded[16:, :].astype(jnp.int32).astype(f32)[:depth]
+    return (values + 32768.0 + (upper * HALF + lower)) * step_of(index)
+
+
+def finish(accs, totals, whole, shares, tiles, place, beta):
     for n in range(tiles):
         rows = slice(n * TILE, (n + 1) * TILE)
         total = jnp.sum(totals[rows, :].T, axis=0, keepdims=True)
@@ -50,10 +85,14 @@
     depth = whole.shape[0] // count
     for k in range(count):
         owner = lax.rem(place + k, count)
-        shares[k][...] = whole[pl.ds(pl.multiple_of(owner * depth, 8), depth), :]
-
-
-def score_kernel(count, first, row, place_ref, model_hbm, *refs):
+        values = whole[pl.ds(pl.multiple_of(owner * depth, 8), depth), :] * beta
+        if k:
+            pack(values, shares[k])
+        else:
+            shares[k][...] = values
+
+
+def score_kernel(count, beta, first, row, place_ref, model_hbm, *refs):
     if first:
         patterns_hbm, refs = refs[0], refs[1:]
     else:
@@ -68,12 +107,13 @@
     whole, totals, model_sems = refs
     rows, pixels = model.shape
     frames = counts.shape[0]
-    steps = pixels // STEP
+    span = STEP if first else min(2 * STEP, pixels)
+    steps = pixels // span
     tiles = rows // TILE
     totals[...] = jnp.zeros_like(totals)
 
     def window(i):
-        return pl.ds(pl.multiple_of(i * STEP, STEP), STEP)
+        return pl.ds(pl.multiple_of(i * span, span), span)
 
     def model_copy(i):
         return pltpu.make_async_copy(
@@ -84,7 +124,7 @@
         slot = lax.rem(i, AHEAD)
         return pltpu.make_async_copy(patterns_hbm.at[:, window(i)], raw.at[slot], raw_sems.at[slot])
 
-    for i in range(AHEAD):
+    for i in range(min(AHEAD, steps)):
         model_copy(i).start()
         if first:
             raw_copy(i).start()
@@ -103,16 +143,16 @@
                 if first:
                     raw_copy(i + AHEAD).start()
 
-            for q in range(STEP // TILE):
-                px = pl.ds(pl.multiple_of(i * STEP + q * TILE, TILE), TILE)
+            for q in range(span // TILE):
+                px = pl.ds(pl.multiple_of(i * span + q * TILE, TILE), TILE)
                 accumulate(model, counts, accs, totals, px, tiles)
 
-        finish(accs, totals, whole, shares, tiles, place_ref[0])
+        finish(accs, totals, whole, shares, tiles, place_ref[0], beta)
 
     pl.run_scoped(scoped, *[pltpu.ACC(j % 2)((frames, TILE), f32) for j in range(2 * tiles)])
 
 
-def partial_scores(place, model, patterns, counts, held, row, rows, pix_count):
+def partial_scores(place, model, patterns, counts, held, row, rows, pix_count, beta):
     pixels = model.shape[1]
     first = counts is None
     frames = patterns.shape[0]
@@ -125,7 +165,9 @@
     else:
         operands = (place, hbm(model), hold(counts), hold(held))
         in_specs = [pl.BlockSpec(memory_space=pltpu.SMEM), anywhere, whole_vmem, anywhere]
-    out_shape = [jax.ShapeDtypeStruct((frames // pix_count, rows), f32)] * pix_count
+    depth = frames // pix_count
+    packed = jax.ShapeDtypeStruct((16 + -(-depth // 16) * 16, rows), jnp.int16)
+    out_shape = [jax.ShapeDtypeStruct((depth, rows), f32)] + [packed] * (pix_count - 1)
     out_shape.append(pltpu.VMEM((rows, pixels), bf16))
     scratch = []
     if first:
@@ -139,7 +181,7 @@
         pltpu.SemaphoreType.DMA((steps,)),
     ]
     return pl.pallas_call(
-        functools.partial(score_kernel, pix_count, first, row),
+        functools.partial(score_kernel, pix_count, beta, first, row),
         out_shape=out_shape,
         in_specs=in_specs,
         out_specs=[whole_vmem] * (len(out_shape) - 1) + [whole_vmem if first else anywhere],
@@ -149,23 +191,24 @@
     )(*operands)
 
 
-def join_kernel(count, beta, *refs):
-    total = refs[0][...]
-    for part in refs[1:count]:
-        total = total + part[...]
-    refs[-1][...] = total * beta
-
-
-def stats_kernel(count, beta, first, *refs):
+def add_up(parts):
+    total = parts[0][...]
+    for part in parts[1:]:
+        total = total + unpack(part, total.shape[0])
+    return total
+
+
+def join_kernel(count, *refs):
+    refs[-1][...] = add_up(refs[:count])
+
+
+def stats_kernel(count, first, *refs):
     parts = refs[:count]
     weights, stat = refs[-3], refs[-2]
     whole = refs[-1]
-    total = parts[0][...]
-    for part in parts[1:]:
-        total = total + part[...]
     start = first.shape[1]
     whole[:, :start] = first[...]
-    whole[:, start:] = total * beta
+    whole[:, start:] = add_up(parts)
     values = whole[...]
     highest = jnp.max(values, axis=1, keepdims=True)
     scaled = jnp.exp(values - highest)
@@ -268,13 +311,14 @@
     rows, wide = across.shape
     whole_vmem = pl.BlockSpec(memory_space=pltpu.VMEM)
     pinned = [hold(a) for a in (counts, *models)]
+    wide_step = min(2 * STEP, pixels)
     return pl.pallas_call(
         functools.partial(update_kernel, len(factors), len(models)),
         out_shape=jax.ShapeDtypeStruct((rows, pixels), bf16),
-        grid=(pixels // STEP,),
+        grid=(pixels // wide_step,),
         in_specs=[pl.BlockSpec(memory_space=pltpu.SMEM)]
         + [whole_vmem] * (1 + len(factors) + len(pinned)),
-        out_specs=pl.BlockSpec((rows, STEP), lambda i: (0, i)),
+        out_specs=pl.BlockSpec((rows, wide_step), lambda i: (0, i)),
         scratch_shapes=[
             pltpu.VMEM((wide, 128), f32),
             pltpu.VMEM((rows, wide), bf16),
@@ -293,20 +337,20 @@
     rows = model.shape[0]
     depth = patterns.shape[0] // pix_count
     head = max(TILE, rows // 3 * 2 // TILE * TILE)
-    *sent, model_a, counts = partial_scores(place, model, patterns, None, None, 0, head, pix_count)
+    *sent, model_a, counts = partial_scores(place, model, patterns, None, None, 0, head, pix_count, beta)
     pieces = [sent[0]] + [shift(sent[k], k, pix_count) for k in range(1, pix_count)]
     *sent, model_b, model_a = partial_scores(
-        place, model, patterns, counts, model_a, head, rows - head, pix_count
+        place, model, patterns, counts, model_a, head, rows - head, pix_count, beta
     )
     first = pl.pallas_call(
-        functools.partial(join_kernel, pix_count, beta),
+        functools.partial(join_kernel, pix_count),
         out_shape=jax.ShapeDtypeStruct((depth, head), f32),
         compiler_params=params(8),
         cost_estimate=pl.CostEstimate(flops=20 * 10**9, bytes_accessed=0, transcendentals=0),
     )(*pieces)
     pieces = [sent[0]] + [shift(sent[k], k, pix_count) for k in range(1, pix_count)]
     weights, stat, model_a, model_b, counts = pl.pallas_call(
-        functools.partial(pass_stats, pix_count, beta),
+        functools.partial(pass_stats, pix_count),
         out_shape=[
             jax.ShapeDtypeStruct((depth, rows), bf16),
             jax.ShapeDtypeStruct((8, depth), f32),
@@ -359,9 +403,9 @@
     )(*small, *[hold(x) for x in held])
 
 
-def pass_stats(count, beta, *refs):
+def pass_stats(count, *refs):
     ins, outs = refs[: count + 4], refs[count + 4 :]
-    stats_kernel(count, beta, ins[count], *ins[:count], outs[0], outs[1], outs[-1])
+    stats_kernel(count, ins[count], *ins[:count], outs[0], outs[1], outs[-1])
 
 
 def solution(mesh):

time: 88.2 us -> 82.3 us (0.933)
  waiting for transfers between devices: 13.1 us -> 7.26 us
    ppermute x12, waiting for transfers between devices: 9.23 us -> 3.45 us  [shift(): return lax.ppermute(x, 'pix', [(i, (i + k) % count) for i in range(count)])]
    pallas_call x1, Pallas kernels: 19.7 us -> 18.3 us  [update(): pl.pallas_call(functools.partial(update_kernel, len(factors), len(models)...]
    pallas_call x4, Pallas kernels: 28.9 us -> 30.2 us  [the longest x2 29.2 us: partial_scores(): pl.pallas_call(functools.partial(score_kernel, pix_count, beta, first, ro...]
  transfers between devices with their start and end apart: 16 -> 16, of which waited for: 8 -> 6; matrix products, arithmetic and copies ran while one was open for 0% -> 0% of each run, Pallas kernels for 13% -> 14%
where the time goes in v3:
time: 82.3 us; the launch traced here: 82.1 us
  Pallas kernels  49.5 us (60%)
  starting transfers between devices  25.3 us (31%)
  waiting for transfers between devices  7.26 us (9%)
    pallas_call x2, Pallas kernels, partial_scores(): pl.pallas_call(functools.partial(score_kernel, pix_count, beta, first, ro...  29.2 us
    ppermute x12, starting transfers between devices, shift(): return lax.ppermute(x, 'pix', [(i, (i + k) % count) for i in range(count)])  19.7 us
    pallas_call x1, Pallas kernels, update(): pl.pallas_call(functools.partial(update_kernel, len(factors), len(models)...  18.3 us
    ppermute x4, starting transfers between devices, swap(): return lax.ppermute(x, 'orient', [(i, i ^ distance) for i in range(count)])  5.54 us
    ppermute x4, waiting for transfers between devices, swap(): return lax.ppermute(x, 'orient', [(i, i ^ distance) for i in range(count)])  3.81 us
    ppermute x12, waiting for transfers between devices, shift(): return lax.ppermute(x, 'pix', [(i, (i + k) % count) for i in range(count)])  3.45 us
  transfers between devices with their start and end apart: 16, of which 6 were waited for; matrix products, arithmetic and copies ran while one was open for 0% of the time, Pallas kernels for 14%

profile of v3, /device:TPU:0, one launch (start us, length us, event | category | flops | bytes accessed | tf_op | source)
XLA Modules:
  0.0 82.1 jit_solution(761044796699944260)
XLA Ops:
  0.0 0.1 pad_add_fusion.place_ref
  0.1 19.1 %shard_map.28 = (f32[96,512]{1,0:T(8,128)S(1)}, s16[112,512]{1,0:T(8,128)(2,1)S(1)}, s16[112,512]{1,0:T(8,128)(2,1)S(1)}, s16[112,512]{1,0:T(8,128)(2,1)S(1)}, b...) custom-call(s32[2]{0:T(128)S(1)} %pad_add_fusion.place_ref, bf16[768,16384]{1,0:T(8,128)(2,1)} %model_hbm.3, ...), custom_call_target="tpu_custom_call" | custom-call | tf_op jit(solution)/shard_map/pallas_call | solution.py:183
  19.2 3.1 %collective-permute-start.3 = (s16[112,512]{1,0:T(8,128)(2,1)S(1)}, s16[112,512]{1,0:T(8,128)(2,1)S(1)}, u32[]{:S(2)}, u32[]{:S(2)}) collective-permute-start(s16[112,512]{1,0:T(8,128)(2,1)S(1)} %get-tuple-element.41), channel_id=1, source_target_pairs={{0,1},{1,2},{2,3},{3,0},{4,5},{5,6},{6,7},{7,4},{8,9},{9,10},{10,1... | collective-permute-start | bytes 344072 | tf_op jit(solution)/shard_map/ppermute | solution.py:332
  22.2 2.6 %collective-permute-start.4 = (s16[112,512]{1,0:T(8,128)(2,1)S(1)}, s16[112,512]{1,0:T(8,128)(2,1)S(1)}, u32[]{:S(2)}, u32[]{:S(2)}) collective-permute-start(s16[112,512]{1,0:T(8,128)(2,1)S(1)} %get-tuple-element.42), channel_id=1, source_target_pairs={{0,2},{1,3},{2,0},{3,1},{4,6},{5,7},{6,4},{7,5},{8,10},{9,11},{10,... | collective-permute-start | bytes 344072 | tf_op jit(solution)/shard_map/ppermute | solution.py:332
  24.8 1.3 %collective-permute-start.5 = (s16[112,512]{1,0:T(8,128)(2,1)S(1)}, s16[112,512]{1,0:T(8,128)(2,1)S(1)}, u32[]{:S(2)}, u32[]{:S(2)}) collective-permute-start(s16[112,512]{1,0:T(8,128)(2,1)S(1)} %get-tuple-element.43), channel_id=1, source_target_pairs={{0,3},{1,0},{2,1},{3,2},{4,7},{5,4},{6,5},{7,6},{8,11},{9,8},{10,9... | collective-permute-start | bytes 344072 | tf_op jit(solution)/shard_map/ppermute | solution.py:332
  26.2 10.1 %shard_map.29 = (f32[96,256]{1,0:T(8,128)S(1)}, s16[112,256]{1,0:T(8,128)(2,1)S(1)}, s16[112,256]{1,0:T(8,128)(2,1)S(1)}, s16[112,256]{1,0:T(8,128)(2,1)S(1)}, b...) custom-call(s32[2]{0:T(128)S(1)} %pad_add_fusion.place_ref, ...), custom_call_target="tpu_custom_call", output_to_operand_aliasing={{5}: (3, {})} | custom-call | tf_op jit(solution)/shard_map/pallas_call | solution.py:183
  36.3 0.7 collective-permute-start
  37.0 0.3 collective-permute-start.1
  37.4 0.0 collective-permute-done.3.refs_1_
  37.4 2.8 %collective-permute-start.2 = (s16[112,256]{1,0:T(8,128)(2,1)S(1)}, s16[112,256]{1,0:T(8,128)(2,1)S(1)}, u32[]{:S(2)}, u32[]{:S(2)}) collective-permute-start(s16[112,256]{1,0:T(8,128)(2,1)S(1)} %get-tuple-element.39), channel_id=1, source_target_pairs={{0,3},{1,0},{2,1},{3,2},{4,7},{5,4},{6,5},{7,6},{8,11},{9,8},{10,9... | collective-permute-start | bytes 172040 | tf_op jit(solution)/shard_map/ppermute | solution.py:332
  40.2 0.0 collective-permute-done.4.refs_2_
  40.2 0.0 collective-permute-done.5.refs_3_
  40.2 0.4 shard_map.30.refs_4_
  40.6 1.8 %collective-permute-done.refs_1_ = s16[112,256]{1,0:T(8,128)(2,1)S(1)} collective-permute-done((s16[112,256]{1,0:T(8,128)(2,1)S(1)}, s16[112,256]{1,0:T(8,128)(2,1)S(1)}, u32[]{:S(2)}, u32[]{:S(2)}) %collective-permute-start) | collective-permute-done | bytes 57376 | tf_op jit(solution)/shard_map/ppermute | solution.py:332
  42.4 1.2 %collective-permute-done.1.refs_2_ = s16[112,256]{1,0:T(8,128)(2,1)S(1)} collective-permute-done((s16[112,256]{1,0:T(8,128)(2,1)S(1)}, s16[112,256]{1,0:T(8,128)(2,1)S(1)}, u32[]{:S(2)}, u32[]{:S(2)}) %collective-permute-start.1) | collective-permute-done | bytes 57376 | tf_op jit(solution)/shard_map/ppermute | solution.py:332
  43.7 0.0 collective-permute-done.2.refs_3_
  43.7 0.6 shard_map.31
  44.2 1.3 %collective-permute-start.6 = (bf16[96,768]{1,0:T(8,128)(2,1)S(1)}, bf16[96,768]{1,0:T(8,128)(2,1)S(1)}, u32[]{:S(2)}, u32[]{:S(2)}) collective-permute-start(bf16[96,768]{1,0:T(8,128)(2,1)S(1)} %get-tuple-element.46.refs_0_), channel_id=1, source_target_pairs={{0,1},{1,2},{2,3},{3,0},{4,5},{5,6},{6,7},{7,4},{8,9},{9,10},{10,1... | collective-permute-start | bytes 442376 | tf_op jit(solution)/shard_map/ppermute | solution.py:332
  45.5 1.8 %collective-permute-start.7 = (bf16[96,768]{1,0:T(8,128)(2,1)S(1)}, bf16[96,768]{1,0:T(8,128)(2,1)S(1)}, u32[]{:S(2)}, u32[]{:S(2)}) collective-permute-start(bf16[96,768]{1,0:T(8,128)(2,1)S(1)} %get-tuple-element.46.refs_0_), channel_id=1, source_target_pairs={{0,2},{1,3},{2,0},{3,1},{4,6},{5,7},{6,4},{7,5},{8,10},{9,11},{10,... | collective-permute-start | bytes 442376 | tf_op jit(solution)/shard_map/ppermute | solution.py:332
  47.3 0.8 collective-permute-start.8
  48.1 0.0 collective-permute-start.9
  48.1 1.2 %collective-permute-done.9.refs_1_ = f32[8,96]{1,0:T(8,128)S(1)} collective-permute-done((f32[8,96]{1,0:T(8,128)S(1)}, f32[8,96]{1,0:T(8,128)S(1)}, u32[]{:S(2)}, u32[]{:S(2)}) %collective-permute-start.9) | collective-permute-done | bytes 3104 | tf_op jit(solution)/shard_map/ppermute | solution.py:377
  49.3 1.6 %collective-permute-start.10 = (f32[8,96]{1,0:T(8,128)S(1)}, f32[8,96]{1,0:T(8,128)S(1)}, u32[]{:S(2)}, u32[]{:S(2)}) collective-permute-start(f32[8,96]{1,0:T(8,128)S(1)} %get-tuple-element.51.refs_0_), channel_id=1, source_target_pairs={{0,8},{4,12},{8,0},{12,4},{16,24},{20,28},{24,16},{28,20},{1,9},{5... | collective-permute-start | bytes 9224 | tf_op jit(solution)/shard_map/ppermute | solution.py:377
  50.8 1.5 %collective-permute-start.11 = (f32[8,96]{1,0:T(8,128)S(1)}, f32[8,96]{1,0:T(8,128)S(1)}, u32[]{:S(2)}, u32[]{:S(2)}) collective-permute-start(f32[8,96]{1,0:T(8,128)S(1)} %get-tuple-element.51.refs_0_), channel_id=1, source_target_pairs={{0,16},{4,20},{8,24},{12,28},{16,0},{20,4},{24,8},{28,12},{1,17},{... | collective-permute-start | bytes 9224 | tf_op jit(solution)/shard_map/ppermute | solution.py:377
  52.3 0.6 collective-permute-done.10.refs_1_
  52.9 2.5 %collective-permute-start.12 = (f32[8,96]{1,0:T(8,128)S(1)}, f32[8,96]{1,0:T(8,128)S(1)}, u32[]{:S(2)}, u32[]{:S(2)}) collective-permute-start(f32[8,96]{1,0:T(8,128)S(1)} %get-tuple-element.51.refs_0_), channel_id=1, source_target_pairs={{0,24},{4,28},{8,16},{12,20},{16,8},{20,12},{24,0},{28,4},{1,25},{... | collective-permute-start | bytes 9224 | tf_op jit(solution)/shard_map/ppermute | solution.py:377
  55.4 0.0 collective-permute-done.11.refs_2_
  55.4 2.1 %collective-permute-done.12.refs_3_ = f32[8,96]{1,0:T(8,128)S(1)} collective-permute-done((f32[8,96]{1,0:T(8,128)S(1)}, f32[8,96]{1,0:T(8,128)S(1)}, u32[]{:S(2)}, u32[]{:S(2)}) %collective-permute-start.12) | collective-permute-done | bytes 3104 | tf_op jit(solution)/shard_map/ppermute | solution.py:377
  57.5 1.3 %collective-permute-start.13 = (f32[8,96]{1,0:T(8,128)S(1)}, f32[8,96]{1,0:T(8,128)S(1)}, u32[]{:S(2)}, u32[]{:S(2)}) collective-permute-start(f32[8,96]{1,0:T(8,128)S(1)} %get-tuple-element.59.refs_0_), channel_id=1, source_target_pairs={{0,1},{1,2},{2,3},{3,0},{4,5},{5,6},{6,7},{7,4},{8,9},{9,10},{10,1... | collective-permute-start | bytes 9224 | tf_op jit(solution)/shard_map/ppermute | solution.py:332
  58.8 1.1 %collective-permute-start.14 = (f32[8,96]{1,0:T(8,128)S(1)}, f32[8,96]{1,0:T(8,128)S(1)}, u32[]{:S(2)}, u32[]{:S(2)}) collective-permute-start(f32[8,96]{1,0:T(8,128)S(1)} %get-tuple-element.59.refs_0_), channel_id=1, source_target_pairs={{0,2},{1,3},{2,0},{3,1},{4,6},{5,7},{6,4},{7,5},{8,10},{9,11},{10,... | collective-permute-start | bytes 9224 | tf_op jit(solution)/shard_map/ppermute | solution.py:332
  59.9 0.0 collective-permute-done.6.refs_1_
  59.9 2.6 %collective-permute-start.15 = (f32[8,96]{1,0:T(8,128)S(1)}, f32[8,96]{1,0:T(8,128)S(1)}, u32[]{:S(2)}, u32[]{:S(2)}) collective-permute-start(f32[8,96]{1,0:T(8,128)S(1)} %get-tuple-element.59.refs_0_), channel_id=1, source_target_pairs={{0,3},{1,0},{2,1},{3,2},{4,7},{5,4},{6,5},{7,6},{8,11},{9,8},{10,9... | collective-permute-start | bytes 9224 | tf_op jit(solution)/shard_map/ppermute | solution.py:332
  62.5 0.0 collective-permute-done.7.refs_2_
  62.5 0.0 collective-permute-done.8.refs_3_
  62.5 0.9 %shard_map.34 = (bf16[768,512]{1,0:T(8,128)(2,1)S(1)}, bf16[512,16384]{1,0:T(8,128)(2,1)S(1)}, bf16[256,16384]{1,0:T(8,128)(2,1)S(1)}, bf16[384,16384]{1,0:T(8,128)(2,1)S(1)}) custom-call(s32[2]{0:T(128)S(1)} %pad_add_fusion.place_ref, bf16[96,768]{1,0:T(8,128)(2,1)S(1)} %get-tuple-element.46.refs_0_, ...), custom_call_target="tpu_custom_call", output_to_operand_aliasing={{1}: (5, {}), {2}: (6, {}), {3}: (7, {})} | custom-call | tf_op jit(solution)/shard_map/pallas_call | solution.py:251
  63.4 0.0 collective-permute-done.13.refs_1_
  63.4 0.0 collective-permute-done.14.refs_2_
  63.4 0.4 collective-permute-done.15.refs_3_
  63.8 18.3 %shard_map.35 = bf16[768,16384]{1,0:T(8,128)(2,1)} custom-call(s32[2]{0:T(128)S(1)} %pad_add_fusion.place_ref, bf16[768,512]{1,0:T(8,128)(2,1)S(1)} %get-tuple-element.58.across, f32[8,96]{1,0:T(8,128)S(1)} %get-tuple-element.59.refs_0_, f32[8,96]{1,0:T(8,128)S(1)} %collective-permute-done.13.refs_1_, f32[8,96]{1,0:T(8,128)S(1)} %collective-permute-done.14.refs_2_, ...), custom_call_target="tpu_custom_call" | custom-call | tf_op jit(solution)/shard_map/pallas_call | solution.py:315
  (2 shorter events, 0.0 us)
Async XLA Ops:
  19.2 18.2 %collective-permute-start.3 = (s16[112,512]{1,0:T(8,128)(2,1)S(1)}, s16[112,512]{1,0:T(8,128)(2,1)S(1)}, u32[]{:S(2)}, u32[]{:S(2)}) collective-permute-start(s16[112,512]{1,0:T(8,128)(2,1)S(1)} %get-tuple-element.41), channel_id=1, source_target_pairs={{0,1},{1,2},{2,3},{3,0},{4,5},{5,6},{6,7},{7,4},{8,9},{9,10},{10,1... | collective-permute-start | bytes 344072 | tf_op jit(solution)/shard_map/ppermute | solution.py:332
  22.2 17.9 %collective-permute-start.4 = (s16[112,512]{1,0:T(8,128)(2,1)S(1)}, s16[112,512]{1,0:T(8,128)(2,1)S(1)}, u32[]{:S(2)}, u32[]{:S(2)}) collective-permute-start(s16[112,512]{1,0:T(8,128)(2,1)S(1)} %get-tuple-element.42), channel_id=1, source_target_pairs={{0,2},{1,3},{2,0},{3,1},{4,6},{5,7},{6,4},{7,5},{8,10},{9,11},{10,... | collective-permute-start | bytes 344072 | tf_op jit(solution)/shard_map/ppermute | solution.py:332
  24.8 15.4 %collective-permute-start.5 = (s16[112,512]{1,0:T(8,128)(2,1)S(1)}, s16[112,512]{1,0:T(8,128)(2,1)S(1)}, u32[]{:S(2)}, u32[]{:S(2)}) collective-permute-start(s16[112,512]{1,0:T(8,128)(2,1)S(1)} %get-tuple-element.43), channel_id=1, source_target_pairs={{0,3},{1,0},{2,1},{3,2},{4,7},{5,4},{6,5},{7,6},{8,11},{9,8},{10,9... | collective-permute-start | bytes 344072 | tf_op jit(solution)/shard_map/ppermute | solution.py:332
  36.3 6.1 %collective-permute-start = (s16[112,256]{1,0:T(8,128)(2,1)S(1)}, s16[112,256]{1,0:T(8,128)(2,1)S(1)}, u32[]{:S(2)}, u32[]{:S(2)}) collective-permute-start(s16[112,256]{1,0:T(8,128)(2,1)S(1)} %get-tuple-element.37), channel_id=1, source_target_pairs={{0,1},{1,2},{2,3},{3,0},{4,5},{5,6},{6,7},{7,4},{8,9},{9,10},{10,1... | collective-permute-start | bytes 172040 | tf_op jit(solution)/shard_map/ppermute | solution.py:332
  37.0 6.6 %collective-permute-start.1 = (s16[112,256]{1,0:T(8,128)(2,1)S(1)}, s16[112,256]{1,0:T(8,128)(2,1)S(1)}, u32[]{:S(2)}, u32[]{:S(2)}) collective-permute-start(s16[112,256]{1,0:T(8,128)(2,1)S(1)} %get-tuple-element.38), channel_id=1, source_target_pairs={{0,2},{1,3},{2,0},{3,1},{4,6},{5,7},{6,4},{7,5},{8,10},{9,11},{10,... | collective-permute-start | bytes 172040 | tf_op jit(solution)/shard_map/ppermute | solution.py:332
  37.4 6.3 %collective-permute-start.2 = (s16[112,256]{1,0:T(8,128)(2,1)S(1)}, s16[112,256]{1,0:T(8,128)(2,1)S(1)}, u32[]{:S(2)}, u32[]{:S(2)}) collective-permute-start(s16[112,256]{1,0:T(8,128)(2,1)S(1)} %get-tuple-element.39), channel_id=1, source_target_pairs={{0,3},{1,0},{2,1},{3,2},{4,7},{5,4},{6,5},{7,6},{8,11},{9,8},{10,9... | collective-permute-start | bytes 172040 | tf_op jit(solution)/shard_map/ppermute | solution.py:332
  44.2 15.7 %collective-permute-start.6 = (bf16[96,768]{1,0:T(8,128)(2,1)S(1)}, bf16[96,768]{1,0:T(8,128)(2,1)S(1)}, u32[]{:S(2)}, u32[]{:S(2)}) collective-permute-start(bf16[96,768]{1,0:T(8,128)(2,1)S(1)} %get-tuple-element.46.refs_0_), channel_id=1, source_target_pairs={{0,1},{1,2},{2,3},{3,0},{4,5},{5,6},{6,7},{7,4},{8,9},{9,10},{10,1... | collective-permute-start | bytes 442376 | tf_op jit(solution)/shard_map/ppermute | solution.py:332
  45.5 17.0 %collective-permute-start.7 = (bf16[96,768]{1,0:T(8,128)(2,1)S(1)}, bf16[96,768]{1,0:T(8,128)(2,1)S(1)}, u32[]{:S(2)}, u32[]{:S(2)}) collective-permute-start(bf16[96,768]{1,0:T(8,128)(2,1)S(1)} %get-tuple-element.46.refs_0_), channel_id=1, source_target_pairs={{0,2},{1,3},{2,0},{3,1},{4,6},{5,7},{6,4},{7,5},{8,10},{9,11},{10,... | collective-permute-start | bytes 442376 | tf_op jit(solution)/shard_map/ppermute | solution.py:332
  47.3 15.2 %collective-permute-start.8 = (bf16[96,768]{1,0:T(8,128)(2,1)S(1)}, bf16[96,768]{1,0:T(8,128)(2,1)S(1)}, u32[]{:S(2)}, u32[]{:S(2)}) collective-permute-start(bf16[96,768]{1,0:T(8,128)(2,1)S(1)} %get-tuple-element.46.refs_0_), channel_id=1, source_target_pairs={{0,3},{1,0},{2,1},{3,2},{4,7},{5,4},{6,5},{7,6},{8,11},{9,8},{10,9... | collective-permute-start | bytes 442376 | tf_op jit(solution)/shard_map/ppermute | solution.py:332
  48.1 1.2 %collective-permute-start.9 = (f32[8,96]{1,0:T(8,128)S(1)}, f32[8,96]{1,0:T(8,128)S(1)}, u32[]{:S(2)}, u32[]{:S(2)}) collective-permute-start(f32[8,96]{1,0:T(8,128)S(1)} %get-tuple-element.47.refs_0_.refs_4_), channel_id=1, source_target_pairs={{0,4},{4,0},{8,12},{12,8},{16,20},{20,16},{24,28},{28,24},{1,5},{5... | collective-permute-start | bytes 9224 | tf_op jit(solution)/shard_map/ppermute | solution.py:377
  49.3 3.7 %collective-permute-start.10 = (f32[8,96]{1,0:T(8,128)S(1)}, f32[8,96]{1,0:T(8,128)S(1)}, u32[]{:S(2)}, u32[]{:S(2)}) collective-permute-start(f32[8,96]{1,0:T(8,128)S(1)} %get-tuple-element.51.refs_0_), channel_id=1, source_target_pairs={{0,8},{4,12},{8,0},{12,4},{16,24},{20,28},{24,16},{28,20},{1,9},{5... | collective-permute-start | bytes 9224 | tf_op jit(solution)/shard_map/ppermute | solution.py:377
  50.8 4.6 %collective-permute-start.11 = (f32[8,96]{1,0:T(8,128)S(1)}, f32[8,96]{1,0:T(8,128)S(1)}, u32[]{:S(2)}, u32[]{:S(2)}) collective-permute-start(f32[8,96]{1,0:T(8,128)S(1)} %get-tuple-element.51.refs_0_), channel_id=1, source_target_pairs={{0,16},{4,20},{8,24},{12,28},{16,0},{20,4},{24,8},{28,12},{1,17},{... | collective-permute-start | bytes 9224 | tf_op jit(solution)/shard_map/ppermute | solution.py:377
  52.9 4.5 %collective-permute-start.12 = (f32[8,96]{1,0:T(8,128)S(1)}, f32[8,96]{1,0:T(8,128)S(1)}, u32[]{:S(2)}, u32[]{:S(2)}) collective-permute-start(f32[8,96]{1,0:T(8,128)S(1)} %get-tuple-element.51.refs_0_), channel_id=1, source_target_pairs={{0,24},{4,28},{8,16},{12,20},{16,8},{20,12},{24,0},{28,4},{1,25},{... | collective-permute-start | bytes 9224 | tf_op jit(solution)/shard_map/ppermute | solution.py:377
  57.5 5.9 %collective-permute-start.13 = (f32[8,96]{1,0:T(8,128)S(1)}, f32[8,96]{1,0:T(8,128)S(1)}, u32[]{:S(2)}, u32[]{:S(2)}) collective-permute-start(f32[8,96]{1,0:T(8,128)S(1)} %get-tuple-element.59.refs_0_), channel_id=1, source_target_pairs={{0,1},{1,2},{2,3},{3,0},{4,5},{5,6},{6,7},{7,4},{8,9},{9,10},{10,1... | collective-permute-start | bytes 9224 | tf_op jit(solution)/shard_map/ppermute | solution.py:332
  58.8 4.6 %collective-permute-start.14 = (f32[8,96]{1,0:T(8,128)S(1)}, f32[8,96]{1,0:T(8,128)S(1)}, u32[]{:S(2)}, u32[]{:S(2)}) collective-permute-start(f32[8,96]{1,0:T(8,128)S(1)} %get-tuple-element.59.refs_0_), channel_id=1, source_target_pairs={{0,2},{1,3},{2,0},{3,1},{4,6},{5,7},{6,4},{7,5},{8,10},{9,11},{10,... | collective-permute-start | bytes 9224 | tf_op jit(solution)/shard_map/ppermute | solution.py:332
  59.9 3.9 %collective-permute-start.15 = (f32[8,96]{1,0:T(8,128)S(1)}, f32[8,96]{1,0:T(8,128)S(1)}, u32[]{:S(2)}, u32[]{:S(2)}) collective-permute-start(f32[8,96]{1,0:T(8,128)S(1)} %get-tuple-element.59.refs_0_), channel_id=1, source_target_pairs={{0,3},{1,0},{2,1},{3,2},{4,7},{5,4},{6,5},{7,6},{8,11},{9,8},{10,9... | collective-permute-start | bytes 9224 | tf_op jit(solution)/shard_map/ppermute | solution.py:332

commit v4 on v3

--- a/solution.py
+++ b/solution.py
@@ -234,9 +234,6 @@
     shares = refs[:count]
     across, stacked = refs[count + 3], refs[-1]
     depth = shares[0].shape[0]
-    wide = stacked.shape[0]
-    if wide > depth * count:
-        stacked[depth * count :, :] = jnp.zeros((wide - depth * count, stacked.shape[1]), f32)
     for k in range(count):
         owner = lax.rem(place_ref[0] + count - k, count)
         stacked[pl.ds(pl.multiple_of(owner * depth, 8), depth), :] = shares[k][...].astype(f32)
@@ -247,15 +244,15 @@
     held = [model_a, model_b, counts]
     count = len(shares)
     depth, rows = shares[0].shape
-    wide = -(-depth * count // TILE) * TILE
+    frames = depth * count
     return pl.pallas_call(
         functools.partial(turn_kernel, count),
-        out_shape=[jax.ShapeDtypeStruct((rows, wide), bf16)] + [held_shape(x) for x in held],
+        out_shape=[jax.ShapeDtypeStruct((rows, frames), bf16)] + [held_shape(x) for x in held],
         in_specs=[pl.BlockSpec(memory_space=pltpu.SMEM)]
         + [pl.BlockSpec(memory_space=pltpu.VMEM)] * count
         + [held_spec()] * 3,
         out_specs=[pl.BlockSpec(memory_space=pltpu.VMEM)] + [held_spec()] * 3,
-        scratch_shapes=[pltpu.VMEM((wide, rows), f32)],
+        scratch_shapes=[pltpu.VMEM((frames, rows), f32)],
         input_output_aliases={count + 1 + j: 1 + j for j in range(3)},
         compiler_params=params(8),
     )(place, *shares, *[hold(x) for x in held])
@@ -273,14 +270,15 @@
     @pl.when(step == 0)
     def _():
         if wide > frames:
-            columns[frames:, :] = jnp.zeros((wide - frames, 128), f32)
+            probs[:, frames:] = jnp.zeros((probs.shape[0], wide - frames), bf16)
         for k in range(count):
             owner = lax.rem(place_ref[0] + count - k, count)
             rows = pl.ds(pl.multiple_of(owner * depth, 8), depth)
             columns[rows, :] = jnp.broadcast_to(factors[k][0:1, :], (128, depth)).T
         rounded = (across[...].astype(f32) * columns[...].T[0:1, :]).astype(bf16)
-        probs[...] = rounded
-        inverse[...] = 1.0 / (jnp.sum(rounded.astype(f32), axis=1, keepdims=True) + PRIOR)
+        probs[:, :frames] = rounded
+        total = jnp.sum(rounded.astype(f32), axis=1, keepdims=True) + PRIOR
+        inverse[...] = jnp.broadcast_to(1.0 / total, inverse.shape)
 
     width = out.shape[1]
 
@@ -300,7 +298,7 @@
                 rows = slice(at, at + model.shape[0])
                 at += model.shape[0]
                 out[rows, q * TILE : (q + 1) * TILE] = (
-                    (numerator[rows] + model[:, px].astype(f32)) * inverse[rows, :]
+                    (numerator[rows] + model[:, px].astype(f32)) * jnp.concatenate([inverse[rows, :]] * 2, 1)
                 ).astype(bf16)
 
     pl.run_scoped(scoped, *[pltpu.ACC(j)((out.shape[0], TILE), f32) for j in range(2)])
@@ -308,7 +306,8 @@
 
 def update(place, across, factors, counts, models):
     frames, pixels = counts.shape
-    rows, wide = across.shape
+    rows = across.shape[0]
+    wide = -(-frames // TILE) * TILE
     whole_vmem = pl.BlockSpec(memory_space=pltpu.VMEM)
     pinned = [hold(a) for a in (counts, *models)]
     wide_step = min(2 * STEP, pixels)
@@ -320,9 +319,9 @@
         + [whole_vmem] * (1 + len(factors) + len(pinned)),
         out_specs=pl.BlockSpec((rows, wide_step), lambda i: (0, i)),
         scratch_shapes=[
-            pltpu.VMEM((wide, 128), f32),
+            pltpu.VMEM((frames, 128), f32),
             pltpu.VMEM((rows, wide), bf16),
-            pltpu.VMEM((rows, 1), f32),
+            pltpu.VMEM((rows, 128), f32),
         ],
         compiler_params=params(10),
     )(place, across, *factors, *pinned)

time: 82.3 us -> 81.6 us (level)
  no operation moved by 1% of the time
where the time goes in v4:
time: 81.6 us; the launch traced here: 81.4 us
  Pallas kernels  48.7 us (60%)
  starting transfers between devices  25.3 us (31%)
  waiting for transfers between devices  7.3 us (9%)
    pallas_call x2, Pallas kernels, partial_scores(): pl.pallas_call(functools.partial(score_kernel, pix_count, beta, first, ro...  29.2 us
    ppermute x12, starting transfers between devices, shift(): return lax.ppermute(x, 'pix', [(i, (i + k) % count) for i in range(count)])  19.7 us
    pallas_call x1, Pallas kernels, update(): pl.pallas_call(functools.partial(update_kernel, len(factors), len(models)...  17.6 us
    ppermute x4, starting transfers between devices, swap(): return lax.ppermute(x, 'orient', [(i, i ^ distance) for i in range(count)])  5.54 us
    ppermute x4, waiting for transfers between devices, swap(): return lax.ppermute(x, 'orient', [(i, i ^ distance) for i in range(count)])  3.81 us
    ppermute x12, waiting for transfers between devices, shift(): return lax.ppermute(x, 'pix', [(i, (i + k) % count) for i in range(count)])  3.49 us
  transfers between devices with their start and end apart: 16, of which 6 were waited for; matrix products, arithmetic and copies ran while one was open for 0% of the time, Pallas kernels for 14%

profile of v4, /device:TPU:0, one launch (start us, length us, event | category | flops | bytes accessed | tf_op | source)
XLA Modules:
  0.0 81.4 jit_solution(13628234532010262385)
XLA Ops:
  0.0 0.1 pad_add_fusion.place_ref
  0.1 19.1 %shard_map.28 = (f32[96,512]{1,0:T(8,128)S(1)}, s16[112,512]{1,0:T(8,128)(2,1)S(1)}, s16[112,512]{1,0:T(8,128)(2,1)S(1)}, s16[112,512]{1,0:T(8,128)(2,1)S(1)}, b...) custom-call(s32[2]{0:T(128)S(1)} %pad_add_fusion.place_ref, bf16[768,16384]{1,0:T(8,128)(2,1)} %model_hbm.3, ...), custom_call_target="tpu_custom_call" | custom-call | tf_op jit(solution)/shard_map/pallas_call | solution.py:183
  19.2 3.1 %collective-permute-start.3 = (s16[112,512]{1,0:T(8,128)(2,1)S(1)}, s16[112,512]{1,0:T(8,128)(2,1)S(1)}, u32[]{:S(2)}, u32[]{:S(2)}) collective-permute-start(s16[112,512]{1,0:T(8,128)(2,1)S(1)} %get-tuple-element.41), channel_id=1, source_target_pairs={{0,1},{1,2},{2,3},{3,0},{4,5},{5,6},{6,7},{7,4},{8,9},{9,10},{10,1... | collective-permute-start | bytes 344072 | tf_op jit(solution)/shard_map/ppermute | solution.py:331
  22.2 2.6 %collective-permute-start.4 = (s16[112,512]{1,0:T(8,128)(2,1)S(1)}, s16[112,512]{1,0:T(8,128)(2,1)S(1)}, u32[]{:S(2)}, u32[]{:S(2)}) collective-permute-start(s16[112,512]{1,0:T(8,128)(2,1)S(1)} %get-tuple-element.42), channel_id=1, source_target_pairs={{0,2},{1,3},{2,0},{3,1},{4,6},{5,7},{6,4},{7,5},{8,10},{9,11},{10,... | collective-permute-start | bytes 344072 | tf_op jit(solution)/shard_map/ppermute | solution.py:331
  24.8 1.3 %collective-permute-start.5 = (s16[112,512]{1,0:T(8,128)(2,1)S(1)}, s16[112,512]{1,0:T(8,128)(2,1)S(1)}, u32[]{:S(2)}, u32[]{:S(2)}) collective-permute-start(s16[112,512]{1,0:T(8,128)(2,1)S(1)} %get-tuple-element.43), channel_id=1, source_target_pairs={{0,3},{1,0},{2,1},{3,2},{4,7},{5,4},{6,5},{7,6},{8,11},{9,8},{10,9... | collective-permute-start | bytes 344072 | tf_op jit(solution)/shard_map/ppermute | solution.py:331
  26.2 10.1 %shard_map.29 = (f32[96,256]{1,0:T(8,128)S(1)}, s16[112,256]{1,0:T(8,128)(2,1)S(1)}, s16[112,256]{1,0:T(8,128)(2,1)S(1)}, s16[112,256]{1,0:T(8,128)(2,1)S(1)}, b...) custom-call(s32[2]{0:T(128)S(1)} %pad_add_fusion.place_ref, ...), custom_call_target="tpu_custom_call", output_to_operand_aliasing={{5}: (3, {})} | custom-call | tf_op jit(solution)/shard_map/pallas_call | solution.py:183
  36.3 0.7 collective-permute-start
  37.0 0.3 collective-permute-start.1
  37.4 0.0 collective-permute-done.3.refs_1_
  37.4 2.8 %collective-permute-start.2 = (s16[112,256]{1,0:T(8,128)(2,1)S(1)}, s16[112,256]{1,0:T(8,128)(2,1)S(1)}, u32[]{:S(2)}, u32[]{:S(2)}) collective-permute-start(s16[112,256]{1,0:T(8,128)(2,1)S(1)} %get-tuple-element.39), channel_id=1, source_target_pairs={{0,3},{1,0},{2,1},{3,2},{4,7},{5,4},{6,5},{7,6},{8,11},{9,8},{10,9... | collective-permute-start | bytes 172040 | tf_op jit(solution)/shard_map/ppermute | solution.py:331
  40.2 0.0 collective-permute-done.4.refs_2_
  40.2 0.0 collective-permute-done.5.refs_3_
  40.2 0.4 shard_map.30.refs_4_
  40.6 1.8 %collective-permute-done.refs_1_ = s16[112,256]{1,0:T(8,128)(2,1)S(1)} collective-permute-done((s16[112,256]{1,0:T(8,128)(2,1)S(1)}, s16[112,256]{1,0:T(8,128)(2,1)S(1)}, u32[]{:S(2)}, u32[]{:S(2)}) %collective-permute-start) | collective-permute-done | bytes 57376 | tf_op jit(solution)/shard_map/ppermute | solution.py:331
  42.4 1.2 %collective-permute-done.1.refs_2_ = s16[112,256]{1,0:T(8,128)(2,1)S(1)} collective-permute-done((s16[112,256]{1,0:T(8,128)(2,1)S(1)}, s16[112,256]{1,0:T(8,128)(2,1)S(1)}, u32[]{:S(2)}, u32[]{:S(2)}) %collective-permute-start.1) | collective-permute-done | bytes 57376 | tf_op jit(solution)/shard_map/ppermute | solution.py:331
  43.7 0.0 collective-permute-done.2.refs_3_
  43.7 0.6 shard_map.31
  44.2 1.3 %collective-permute-start.6 = (bf16[96,768]{1,0:T(8,128)(2,1)S(1)}, bf16[96,768]{1,0:T(8,128)(2,1)S(1)}, u32[]{:S(2)}, u32[]{:S(2)}) collective-permute-start(bf16[96,768]{1,0:T(8,128)(2,1)S(1)} %get-tuple-element.46.refs_0_), channel_id=1, source_target_pairs={{0,1},{1,2},{2,3},{3,0},{4,5},{5,6},{6,7},{7,4},{8,9},{9,10},{10,1... | collective-permute-start | bytes 442376 | tf_op jit(solution)/shard_map/ppermute | solution.py:331
  45.5 1.8 %collective-permute-start.7 = (bf16[96,768]{1,0:T(8,128)(2,1)S(1)}, bf16[96,768]{1,0:T(8,128)(2,1)S(1)}, u32[]{:S(2)}, u32[]{:S(2)}) collective-permute-start(bf16[96,768]{1,0:T(8,128)(2,1)S(1)} %get-tuple-element.46.refs_0_), channel_id=1, source_target_pairs={{0,2},{1,3},{2,0},{3,1},{4,6},{5,7},{6,4},{7,5},{8,10},{9,11},{10,... | collective-permute-start | bytes 442376 | tf_op jit(solution)/shard_map/ppermute | solution.py:331
  47.3 0.8 collective-permute-start.8
  48.1 0.0 collective-permute-start.9
  48.1 1.2 %collective-permute-done.9.refs_1_ = f32[8,96]{1,0:T(8,128)S(1)} collective-permute-done((f32[8,96]{1,0:T(8,128)S(1)}, f32[8,96]{1,0:T(8,128)S(1)}, u32[]{:S(2)}, u32[]{:S(2)}) %collective-permute-start.9) | collective-permute-done | bytes 3104 | tf_op jit(solution)/shard_map/ppermute | solution.py:376
  49.3 1.6 %collective-permute-start.10 = (f32[8,96]{1,0:T(8,128)S(1)}, f32[8,96]{1,0:T(8,128)S(1)}, u32[]{:S(2)}, u32[]{:S(2)}) collective-permute-start(f32[8,96]{1,0:T(8,128)S(1)} %get-tuple-element.51.refs_0_), channel_id=1, source_target_pairs={{0,8},{4,12},{8,0},{12,4},{16,24},{20,28},{24,16},{28,20},{1,9},{5... | collective-permute-start | bytes 9224 | tf_op jit(solution)/shard_map/ppermute | solution.py:376
  50.8 1.5 %collective-permute-start.11 = (f32[8,96]{1,0:T(8,128)S(1)}, f32[8,96]{1,0:T(8,128)S(1)}, u32[]{:S(2)}, u32[]{:S(2)}) collective-permute-start(f32[8,96]{1,0:T(8,128)S(1)} %get-tuple-element.51.refs_0_), channel_id=1, source_target_pairs={{0,16},{4,20},{8,24},{12,28},{16,0},{20,4},{24,8},{28,12},{1,17},{... | collective-permute-start | bytes 9224 | tf_op jit(solution)/shard_map/ppermute | solution.py:376
  52.3 0.6 collective-permute-done.10.refs_1_
  52.9 2.5 %collective-permute-start.12 = (f32[8,96]{1,0:T(8,128)S(1)}, f32[8,96]{1,0:T(8,128)S(1)}, u32[]{:S(2)}, u32[]{:S(2)}) collective-permute-start(f32[8,96]{1,0:T(8,128)S(1)} %get-tuple-element.51.refs_0_), channel_id=1, source_target_pairs={{0,24},{4,28},{8,16},{12,20},{16,8},{20,12},{24,0},{28,4},{1,25},{... | collective-permute-start | bytes 9224 | tf_op jit(solution)/shard_map/ppermute | solution.py:376
  55.4 0.0 collective-permute-done.11.refs_2_
  55.4 2.1 %collective-permute-done.12.refs_3_ = f32[8,96]{1,0:T(8,128)S(1)} collective-permute-done((f32[8,96]{1,0:T(8,128)S(1)}, f32[8,96]{1,0:T(8,128)S(1)}, u32[]{:S(2)}, u32[]{:S(2)}) %collective-permute-start.12) | collective-permute-done | bytes 3104 | tf_op jit(solution)/shard_map/ppermute | solution.py:376
  57.5 1.3 %collective-permute-start.13 = (f32[8,96]{1,0:T(8,128)S(1)}, f32[8,96]{1,0:T(8,128)S(1)}, u32[]{:S(2)}, u32[]{:S(2)}) collective-permute-start(f32[8,96]{1,0:T(8,128)S(1)} %get-tuple-element.59.refs_0_), channel_id=1, source_target_pairs={{0,1},{1,2},{2,3},{3,0},{4,5},{5,6},{6,7},{7,4},{8,9},{9,10},{10,1... | collective-permute-start | bytes 9224 | tf_op jit(solution)/shard_map/ppermute | solution.py:331
  58.8 1.1 %collective-permute-start.14 = (f32[8,96]{1,0:T(8,128)S(1)}, f32[8,96]{1,0:T(8,128)S(1)}, u32[]{:S(2)}, u32[]{:S(2)}) collective-permute-start(f32[8,96]{1,0:T(8,128)S(1)} %get-tuple-element.59.refs_0_), channel_id=1, source_target_pairs={{0,2},{1,3},{2,0},{3,1},{4,6},{5,7},{6,4},{7,5},{8,10},{9,11},{10,... | collective-permute-start | bytes 9224 | tf_op jit(solution)/shard_map/ppermute | solution.py:331
  59.9 0.0 collective-permute-done.6.refs_1_
  59.9 2.6 %collective-permute-start.15 = (f32[8,96]{1,0:T(8,128)S(1)}, f32[8,96]{1,0:T(8,128)S(1)}, u32[]{:S(2)}, u32[]{:S(2)}) collective-permute-start(f32[8,96]{1,0:T(8,128)S(1)} %get-tuple-element.59.refs_0_), channel_id=1, source_target_pairs={{0,3},{1,0},{2,1},{3,2},{4,7},{5,4},{6,5},{7,6},{8,11},{9,8},{10,9... | collective-permute-start | bytes 9224 | tf_op jit(solution)/shard_map/ppermute | solution.py:331
  62.5 0.0 collective-permute-done.7.refs_2_
  62.5 0.0 collective-permute-done.8.refs_3_
  62.5 0.9 %shard_map.34 = (bf16[768,384]{1,0:T(8,128)(2,1)S(1)}, bf16[512,16384]{1,0:T(8,128)(2,1)S(1)}, bf16[256,16384]{1,0:T(8,128)(2,1)S(1)}, bf16[384,16384]{1,0:T(8,128)(2,1)S(1)}) custom-call(s32[2]{0:T(128)S(1)} %pad_add_fusion.place_ref, bf16[96,768]{1,0:T(8,128)(2,1)S(1)} %get-tuple-element.46.refs_0_, ...), custom_call_target="tpu_custom_call", output_to_operand_aliasing={{1}: (5, {}), {2}: (6, {}), {3}: (7, {})} | custom-call | tf_op jit(solution)/shard_map/pallas_call | solution.py:248
  63.3 0.0 collective-permute-done.13.refs_1_
  63.3 0.0 collective-permute-done.14.refs_2_
  63.4 0.4 collective-permute-done.15.refs_3_
  63.8 17.6 %shard_map.35 = bf16[768,16384]{1,0:T(8,128)(2,1)} custom-call(s32[2]{0:T(128)S(1)} %pad_add_fusion.place_ref, bf16[768,384]{1,0:T(8,128)(2,1)S(1)} %get-tuple-element.58.across, f32[8,96]{1,0:T(8,128)S(1)} %get-tuple-element.59.refs_0_, f32[8,96]{1,0:T(8,128)S(1)} %collective-permute-done.13.refs_1_, f32[8,96]{1,0:T(8,128)S(1)} %collective-permute-done.14.refs_2_, ...), custom_call_target="tpu_custom_call" | custom-call | tf_op jit(solution)/shard_map/pallas_call | solution.py:314
  (2 shorter events, 0.0 us)
Async XLA Ops:
  19.2 18.2 %collective-permute-start.3 = (s16[112,512]{1,0:T(8,128)(2,1)S(1)}, s16[112,512]{1,0:T(8,128)(2,1)S(1)}, u32[]{:S(2)}, u32[]{:S(2)}) collective-permute-start(s16[112,512]{1,0:T(8,128)(2,1)S(1)} %get-tuple-element.41), channel_id=1, source_target_pairs={{0,1},{1,2},{2,3},{3,0},{4,5},{5,6},{6,7},{7,4},{8,9},{9,10},{10,1... | collective-permute-start | bytes 344072 | tf_op jit(solution)/shard_map/ppermute | solution.py:331
  22.2 17.9 %collective-permute-start.4 = (s16[112,512]{1,0:T(8,128)(2,1)S(1)}, s16[112,512]{1,0:T(8,128)(2,1)S(1)}, u32[]{:S(2)}, u32[]{:S(2)}) collective-permute-start(s16[112,512]{1,0:T(8,128)(2,1)S(1)} %get-tuple-element.42), channel_id=1, source_target_pairs={{0,2},{1,3},{2,0},{3,1},{4,6},{5,7},{6,4},{7,5},{8,10},{9,11},{10,... | collective-permute-start | bytes 344072 | tf_op jit(solution)/shard_map/ppermute | solution.py:331
  24.8 15.4 %collective-permute-start.5 = (s16[112,512]{1,0:T(8,128)(2,1)S(1)}, s16[112,512]{1,0:T(8,128)(2,1)S(1)}, u32[]{:S(2)}, u32[]{:S(2)}) collective-permute-start(s16[112,512]{1,0:T(8,128)(2,1)S(1)} %get-tuple-element.43), channel_id=1, source_target_pairs={{0,3},{1,0},{2,1},{3,2},{4,7},{5,4},{6,5},{7,6},{8,11},{9,8},{10,9... | collective-permute-start | bytes 344072 | tf_op jit(solution)/shard_map/ppermute | solution.py:331
  36.3 6.1 %collective-permute-start = (s16[112,256]{1,0:T(8,128)(2,1)S(1)}, s16[112,256]{1,0:T(8,128)(2,1)S(1)}, u32[]{:S(2)}, u32[]{:S(2)}) collective-permute-start(s16[112,256]{1,0:T(8,128)(2,1)S(1)} %get-tuple-element.37), channel_id=1, source_target_pairs={{0,1},{1,2},{2,3},{3,0},{4,5},{5,6},{6,7},{7,4},{8,9},{9,10},{10,1... | collective-permute-start | bytes 172040 | tf_op jit(solution)/shard_map/ppermute | solution.py:331
  37.0 6.6 %collective-permute-start.1 = (s16[112,256]{1,0:T(8,128)(2,1)S(1)}, s16[112,256]{1,0:T(8,128)(2,1)S(1)}, u32[]{:S(2)}, u32[]{:S(2)}) collective-permute-start(s16[112,256]{1,0:T(8,128)(2,1)S(1)} %get-tuple-element.38), channel_id=1, source_target_pairs={{0,2},{1,3},{2,0},{3,1},{4,6},{5,7},{6,4},{7,5},{8,10},{9,11},{10,... | collective-permute-start | bytes 172040 | tf_op jit(solution)/shard_map/ppermute | solution.py:331
  37.4 6.3 %collective-permute-start.2 = (s16[112,256]{1,0:T(8,128)(2,1)S(1)}, s16[112,256]{1,0:T(8,128)(2,1)S(1)}, u32[]{:S(2)}, u32[]{:S(2)}) collective-permute-start(s16[112,256]{1,0:T(8,128)(2,1)S(1)} %get-tuple-element.39), channel_id=1, source_target_pairs={{0,3},{1,0},{2,1},{3,2},{4,7},{5,4},{6,5},{7,6},{8,11},{9,8},{10,9... | collective-permute-start | bytes 172040 | tf_op jit(solution)/shard_map/ppermute | solution.py:331
  44.2 15.7 %collective-permute-start.6 = (bf16[96,768]{1,0:T(8,128)(2,1)S(1)}, bf16[96,768]{1,0:T(8,128)(2,1)S(1)}, u32[]{:S(2)}, u32[]{:S(2)}) collective-permute-start(bf16[96,768]{1,0:T(8,128)(2,1)S(1)} %get-tuple-element.46.refs_0_), channel_id=1, source_target_pairs={{0,1},{1,2},{2,3},{3,0},{4,5},{5,6},{6,7},{7,4},{8,9},{9,10},{10,1... | collective-permute-start | bytes 442376 | tf_op jit(solution)/shard_map/ppermute | solution.py:331
  45.5 17.0 %collective-permute-start.7 = (bf16[96,768]{1,0:T(8,128)(2,1)S(1)}, bf16[96,768]{1,0:T(8,128)(2,1)S(1)}, u32[]{:S(2)}, u32[]{:S(2)}) collective-permute-start(bf16[96,768]{1,0:T(8,128)(2,1)S(1)} %get-tuple-element.46.refs_0_), channel_id=1, source_target_pairs={{0,2},{1,3},{2,0},{3,1},{4,6},{5,7},{6,4},{7,5},{8,10},{9,11},{10,... | collective-permute-start | bytes 442376 | tf_op jit(solution)/shard_map/ppermute | solution.py:331
  47.3 15.2 %collective-permute-start.8 = (bf16[96,768]{1,0:T(8,128)(2,1)S(1)}, bf16[96,768]{1,0:T(8,128)(2,1)S(1)}, u32[]{:S(2)}, u32[]{:S(2)}) collective-permute-start(bf16[96,768]{1,0:T(8,128)(2,1)S(1)} %get-tuple-element.46.refs_0_), channel_id=1, source_target_pairs={{0,3},{1,0},{2,1},{3,2},{4,7},{5,4},{6,5},{7,6},{8,11},{9,8},{10,9... | collective-permute-start | bytes 442376 | tf_op jit(solution)/shard_map/ppermute | solution.py:331
  48.1 1.2 %collective-permute-start.9 = (f32[8,96]{1,0:T(8,128)S(1)}, f32[8,96]{1,0:T(8,128)S(1)}, u32[]{:S(2)}, u32[]{:S(2)}) collective-permute-start(f32[8,96]{1,0:T(8,128)S(1)} %get-tuple-element.47.refs_0_.refs_4_), channel_id=1, source_target_pairs={{0,4},{4,0},{8,12},{12,8},{16,20},{20,16},{24,28},{28,24},{1,5},{5... | collective-permute-start | bytes 9224 | tf_op jit(solution)/shard_map/ppermute | solution.py:376
  49.3 3.7 %collective-permute-start.10 = (f32[8,96]{1,0:T(8,128)S(1)}, f32[8,96]{1,0:T(8,128)S(1)}, u32[]{:S(2)}, u32[]{:S(2)}) collective-permute-start(f32[8,96]{1,0:T(8,128)S(1)} %get-tuple-element.51.refs_0_), channel_id=1, source_target_pairs={{0,8},{4,12},{8,0},{12,4},{16,24},{20,28},{24,16},{28,20},{1,9},{5... | collective-permute-start | bytes 9224 | tf_op jit(solution)/shard_map/ppermute | solution.py:376
  50.8 4.6 %collective-permute-start.11 = (f32[8,96]{1,0:T(8,128)S(1)}, f32[8,96]{1,0:T(8,128)S(1)}, u32[]{:S(2)}, u32[]{:S(2)}) collective-permute-start(f32[8,96]{1,0:T(8,128)S(1)} %get-tuple-element.51.refs_0_), channel_id=1, source_target_pairs={{0,16},{4,20},{8,24},{12,28},{16,0},{20,4},{24,8},{28,12},{1,17},{... | collective-permute-start | bytes 9224 | tf_op jit(solution)/shard_map/ppermute | solution.py:376
  52.9 4.5 %collective-permute-start.12 = (f32[8,96]{1,0:T(8,128)S(1)}, f32[8,96]{1,0:T(8,128)S(1)}, u32[]{:S(2)}, u32[]{:S(2)}) collective-permute-start(f32[8,96]{1,0:T(8,128)S(1)} %get-tuple-element.51.refs_0_), channel_id=1, source_target_pairs={{0,24},{4,28},{8,16},{12,20},{16,8},{20,12},{24,0},{28,4},{1,25},{... | collective-permute-start | bytes 9224 | tf_op jit(solution)/shard_map/ppermute | solution.py:376
  57.5 5.9 %collective-permute-start.13 = (f32[8,96]{1,0:T(8,128)S(1)}, f32[8,96]{1,0:T(8,128)S(1)}, u32[]{:S(2)}, u32[]{:S(2)}) collective-permute-start(f32[8,96]{1,0:T(8,128)S(1)} %get-tuple-element.59.refs_0_), channel_id=1, source_target_pairs={{0,1},{1,2},{2,3},{3,0},{4,5},{5,6},{6,7},{7,4},{8,9},{9,10},{10,1... | collective-permute-start | bytes 9224 | tf_op jit(solution)/shard_map/ppermute | solution.py:331
  58.8 4.6 %collective-permute-start.14 = (f32[8,96]{1,0:T(8,128)S(1)}, f32[8,96]{1,0:T(8,128)S(1)}, u32[]{:S(2)}, u32[]{:S(2)}) collective-permute-start(f32[8,96]{1,0:T(8,128)S(1)} %get-tuple-element.59.refs_0_), channel_id=1, source_target_pairs={{0,2},{1,3},{2,0},{3,1},{4,6},{5,7},{6,4},{7,5},{8,10},{9,11},{10,... | collective-permute-start | bytes 9224 | tf_op jit(solution)/shard_map/ppermute | solution.py:331
  59.9 3.9 %collective-permute-start.15 = (f32[8,96]{1,0:T(8,128)S(1)}, f32[8,96]{1,0:T(8,128)S(1)}, u32[]{:S(2)}, u32[]{:S(2)}) collective-permute-start(f32[8,96]{1,0:T(8,128)S(1)} %get-tuple-element.59.refs_0_), channel_id=1, source_target_pairs={{0,3},{1,0},{2,1},{3,2},{4,7},{5,4},{6,5},{7,6},{8,11},{9,8},{10,9... | collective-permute-start | bytes 9224 | tf_op jit(solution)/shard_map/ppermute | solution.py:331

commit v5 on v4

--- a/solution.py
+++ b/solution.py
@@ -15,6 +15,7 @@
 STEP = 1024
 TILE = 256
 AHEAD = 3
+EARLY = (2, 1)
 FINEST, STEPS, LEVELS, HALF = -14, 20, 65000.0, 16384.0
 
 
@@ -363,8 +364,10 @@
         input_output_aliases={pix_count + 1 + j: 2 + j for j in range(3)},
         compiler_params=params(8),
     )(*pieces, first, hold(model_a), hold(model_b), hold(counts))
-    shares = [weights] + [shift(weights, k, pix_count) for k in range(1, pix_count)]
-    pair, model_a, model_b, counts = merge([stat, swap(stat, 1, orient_count)], model_a, model_b, counts)
+    pair, model_a, model_b, counts, late = merge(
+        [stat, swap(stat, 1, orient_count)], model_a, model_b, counts, weights=weights
+    )
+    shares = [late] + [shift(weights if k in EARLY else late, k, pix_count) for k in range(1, pix_count)]
     pairs = [pair] + [swap(pair, k, orient_count) for k in range(2, orient_count, 2)]
     factor, model_a, model_b, counts = merge(pairs, model_a, model_b, counts, stat)
     factors = [factor] + [shift(factor, k, pix_count) for k in range(1, pix_count)]
@@ -378,7 +381,7 @@
 
 def merge_kernel(number, last, *refs):
     pairs = refs[:number]
-    out = refs[number + (4 if last else 3)]
+    out = refs[number + 4]
     tops = [pair[0:1, :] for pair in pairs]
     overall = functools.reduce(jnp.maximum, tops)
     total = sum(pair[1:2, :] * jnp.exp(top - overall) for pair, top in zip(pairs, tops))
@@ -387,16 +390,20 @@
     else:
         row = lax.broadcasted_iota(jnp.int32, out.shape, 0)
         out[...] = jnp.where(row == 0, overall, total)
-
-
-def merge(pairs, model_a, model_b, counts, stat=None):
-    small = pairs + ([] if stat is None else [stat])
+        refs[-1][...] = refs[number][...]
+
+
+def merge(pairs, model_a, model_b, counts, stat=None, weights=None):
+    small = pairs + [weights if stat is None else stat]
+    late = [] if weights is None else [jax.ShapeDtypeStruct(weights.shape, weights.dtype)]
     held = [model_a, model_b, counts]
     return pl.pallas_call(
         functools.partial(merge_kernel, len(pairs), stat is not None),
-        out_shape=[jax.ShapeDtypeStruct(pairs[0].shape, f32)] + [held_shape(x) for x in held],
+        out_shape=[jax.ShapeDtypeStruct(pairs[0].shape, f32)] + [held_shape(x) for x in held] + late,
         in_specs=[pl.BlockSpec(memory_space=pltpu.VMEM)] * len(small) + [held_spec()] * 3,
-        out_specs=[pl.BlockSpec(memory_space=pltpu.VMEM)] + [held_spec()] * 3,
+        out_specs=[pl.BlockSpec(memory_space=pltpu.VMEM)]
+        + [held_spec()] * 3
+        + [pl.BlockSpec(memory_space=pltpu.VMEM)] * len(late),
         input_output_aliases={len(small) + j: 1 + j for j in range(3)},
         compiler_params=params(8),
     )(*small, *[hold(x) for x in held])

time: 81.6 us -> 80.5 us (0.987)
  waiting for transfers between devices: 7.3 us -> 6.14 us
    ppermute x4, waiting for transfers between devices: 3.81 us -> 2.65 us  [swap(): return lax.ppermute(x, 'orient', [(i, i ^ distance) for i in range(count)])]
  transfers between devices with their start and end apart: 16 -> 16, of which waited for: 6 -> 5; matrix products, arithmetic and copies ran while one was open for 0% -> 0% of each run, Pallas kernels for 14% -> 14%
where the time goes in v5:
time: 80.5 us; the launch traced here: 80.3 us
  Pallas kernels  48.7 us (60%)
  starting transfers between devices  25.3 us (31%)
  waiting for transfers between devices  6.14 us (8%)
    pallas_call x2, Pallas kernels, partial_scores(): pl.pallas_call(functools.partial(score_kernel, pix_count, beta, first, ro...  29.2 us
    ppermute x12, starting transfers between devices, shift(): return lax.ppermute(x, 'pix', [(i, (i + k) % count) for i in range(count)])  19.8 us
    pallas_call x1, Pallas kernels, update(): pl.pallas_call(functools.partial(update_kernel, len(factors), len(models)...  17.6 us
    ppermute x4, starting transfers between devices, swap(): return lax.ppermute(x, 'orient', [(i, i ^ distance) for i in range(count)])  5.5 us
    ppermute x12, waiting for transfers between devices, shift(): return lax.ppermute(x, 'pix', [(i, (i + k) % count) for i in range(count)])  3.49 us
    ppermute x4, waiting for transfers between devices, swap(): return lax.ppermute(x, 'orient', [(i, i ^ distance) for i in range(count)])  2.65 us
  transfers between devices with their start and end apart: 16, of which 5 were waited for; matrix products, arithmetic and copies ran while one was open for 0% of the time, Pallas kernels for 14%

profile of v5, /device:TPU:0, one launch (start us, length us, event | category | flops | bytes accessed | tf_op | source)
XLA Modules:
  0.0 80.3 jit_solution(6859965706138913216)
XLA Ops:
  0.0 0.1 pad_add_fusion.place_ref
  0.1 19.1 %shard_map.28 = (f32[96,512]{1,0:T(8,128)S(1)}, s16[112,512]{1,0:T(8,128)(2,1)S(1)}, s16[112,512]{1,0:T(8,128)(2,1)S(1)}, s16[112,512]{1,0:T(8,128)(2,1)S(1)}, b...) custom-call(s32[2]{0:T(128)S(1)} %pad_add_fusion.place_ref, bf16[768,16384]{1,0:T(8,128)(2,1)} %model_hbm.3, ...), custom_call_target="tpu_custom_call" | custom-call | tf_op jit(solution)/shard_map/pallas_call | solution.py:184
  19.2 3.1 %collective-permute-start.3 = (s16[112,512]{1,0:T(8,128)(2,1)S(1)}, s16[112,512]{1,0:T(8,128)(2,1)S(1)}, u32[]{:S(2)}, u32[]{:S(2)}) collective-permute-start(s16[112,512]{1,0:T(8,128)(2,1)S(1)} %get-tuple-element.42), channel_id=1, source_target_pairs={{0,1},{1,2},{2,3},{3,0},{4,5},{5,6},{6,7},{7,4},{8,9},{9,10},{10,1... | collective-permute-start | bytes 344072 | tf_op jit(solution)/shard_map/ppermute | solution.py:332
  22.2 2.6 %collective-permute-start.4 = (s16[112,512]{1,0:T(8,128)(2,1)S(1)}, s16[112,512]{1,0:T(8,128)(2,1)S(1)}, u32[]{:S(2)}, u32[]{:S(2)}) collective-permute-start(s16[112,512]{1,0:T(8,128)(2,1)S(1)} %get-tuple-element.43), channel_id=1, source_target_pairs={{0,2},{1,3},{2,0},{3,1},{4,6},{5,7},{6,4},{7,5},{8,10},{9,11},{10,... | collective-permute-start | bytes 344072 | tf_op jit(solution)/shard_map/ppermute | solution.py:332
  24.8 1.3 %collective-permute-start.5 = (s16[112,512]{1,0:T(8,128)(2,1)S(1)}, s16[112,512]{1,0:T(8,128)(2,1)S(1)}, u32[]{:S(2)}, u32[]{:S(2)}) collective-permute-start(s16[112,512]{1,0:T(8,128)(2,1)S(1)} %get-tuple-element.44), channel_id=1, source_target_pairs={{0,3},{1,0},{2,1},{3,2},{4,7},{5,4},{6,5},{7,6},{8,11},{9,8},{10,9... | collective-permute-start | bytes 344072 | tf_op jit(solution)/shard_map/ppermute | solution.py:332
  26.2 10.1 %shard_map.29 = (f32[96,256]{1,0:T(8,128)S(1)}, s16[112,256]{1,0:T(8,128)(2,1)S(1)}, s16[112,256]{1,0:T(8,128)(2,1)S(1)}, s16[112,256]{1,0:T(8,128)(2,1)S(1)}, b...) custom-call(s32[2]{0:T(128)S(1)} %pad_add_fusion.place_ref, ...), custom_call_target="tpu_custom_call", output_to_operand_aliasing={{5}: (3, {})} | custom-call | tf_op jit(solution)/shard_map/pallas_call | solution.py:184
  36.3 0.7 collective-permute-start
  37.0 0.3 collective-permute-start.1
  37.4 0.0 collective-permute-done.3.refs_1_
  37.4 2.8 %collective-permute-start.2 = (s16[112,256]{1,0:T(8,128)(2,1)S(1)}, s16[112,256]{1,0:T(8,128)(2,1)S(1)}, u32[]{:S(2)}, u32[]{:S(2)}) collective-permute-start(s16[112,256]{1,0:T(8,128)(2,1)S(1)} %get-tuple-element.40), channel_id=1, source_target_pairs={{0,3},{1,0},{2,1},{3,2},{4,7},{5,4},{6,5},{7,6},{8,11},{9,8},{10,9... | collective-permute-start | bytes 172040 | tf_op jit(solution)/shard_map/ppermute | solution.py:332
  40.2 0.0 collective-permute-done.4.refs_2_
  40.2 0.0 collective-permute-done.5.refs_3_
  40.2 0.4 shard_map.30.refs_4_
  40.6 1.8 %collective-permute-done.refs_1_ = s16[112,256]{1,0:T(8,128)(2,1)S(1)} collective-permute-done((s16[112,256]{1,0:T(8,128)(2,1)S(1)}, s16[112,256]{1,0:T(8,128)(2,1)S(1)}, u32[]{:S(2)}, u32[]{:S(2)}) %collective-permute-start) | collective-permute-done | bytes 57376 | tf_op jit(solution)/shard_map/ppermute | solution.py:332
  42.4 1.2 %collective-permute-done.1.refs_2_ = s16[112,256]{1,0:T(8,128)(2,1)S(1)} collective-permute-done((s16[112,256]{1,0:T(8,128)(2,1)S(1)}, s16[112,256]{1,0:T(8,128)(2,1)S(1)}, u32[]{:S(2)}, u32[]{:S(2)}) %collective-permute-start.1) | collective-permute-done | bytes 57376 | tf_op jit(solution)/shard_map/ppermute | solution.py:332
  43.7 0.0 collective-permute-done.2.refs_3_
  43.7 0.6 shard_map.31
  44.2 0.0 collective-permute-start.6
  44.3 1.3 %collective-permute-start.7 = (bf16[96,768]{1,0:T(8,128)(2,1)S(1)}, bf16[96,768]{1,0:T(8,128)(2,1)S(1)}, u32[]{:S(2)}, u32[]{:S(2)}) collective-permute-start(bf16[96,768]{1,0:T(8,128)(2,1)S(1)} %get-tuple-element.48.refs_2_), channel_id=1, source_target_pairs={{0,1},{1,2},{2,3},{3,0},{4,5},{5,6},{6,7},{7,4},{8,9},{9,10},{10,1... | collective-permute-start | bytes 442376 | tf_op jit(solution)/shard_map/ppermute | solution.py:332
  45.6 1.8 %collective-permute-start.8 = (bf16[96,768]{1,0:T(8,128)(2,1)S(1)}, bf16[96,768]{1,0:T(8,128)(2,1)S(1)}, u32[]{:S(2)}, u32[]{:S(2)}) collective-permute-start(bf16[96,768]{1,0:T(8,128)(2,1)S(1)} %get-tuple-element.48.refs_2_), channel_id=1, source_target_pairs={{0,2},{1,3},{2,0},{3,1},{4,6},{5,7},{6,4},{7,5},{8,10},{9,11},{10,... | collective-permute-start | bytes 442376 | tf_op jit(solution)/shard_map/ppermute | solution.py:332
  47.4 0.0 collective-permute-done.6.refs_1_
  47.4 0.8 %collective-permute-start.9 = (bf16[96,768]{1,0:T(8,128)(2,1)S(1)}, bf16[96,768]{1,0:T(8,128)(2,1)S(1)}, u32[]{:S(2)}, u32[]{:S(2)}) collective-permute-start(bf16[96,768]{1,0:T(8,128)(2,1)S(1)} %get-tuple-element.52.refs_0_), channel_id=1, source_target_pairs={{0,3},{1,0},{2,1},{3,2},{4,7},{5,4},{6,5},{7,6},{8,11},{9,8},{10,9... | collective-permute-start | bytes 442376 | tf_op jit(solution)/shard_map/ppermute | solution.py:332
  48.2 1.5 %collective-permute-start.10 = (f32[8,96]{1,0:T(8,128)S(1)}, f32[8,96]{1,0:T(8,128)S(1)}, u32[]{:S(2)}, u32[]{:S(2)}) collective-permute-start(f32[8,96]{1,0:T(8,128)S(1)} %get-tuple-element.53.refs_0_), channel_id=1, source_target_pairs={{0,8},{4,12},{8,0},{12,4},{16,24},{20,28},{24,16},{28,20},{1,9},{5... | collective-permute-start | bytes 9224 | tf_op jit(solution)/shard_map/ppermute | solution.py:379
  49.7 1.5 %collective-permute-start.11 = (f32[8,96]{1,0:T(8,128)S(1)}, f32[8,96]{1,0:T(8,128)S(1)}, u32[]{:S(2)}, u32[]{:S(2)}) collective-permute-start(f32[8,96]{1,0:T(8,128)S(1)} %get-tuple-element.53.refs_0_), channel_id=1, source_target_pairs={{0,16},{4,20},{8,24},{12,28},{16,0},{20,4},{24,8},{28,12},{1,17},{... | collective-permute-start | bytes 9224 | tf_op jit(solution)/shard_map/ppermute | solution.py:379
  51.2 0.6 collective-permute-done.10.refs_1_
  51.8 2.5 %collective-permute-start.12 = (f32[8,96]{1,0:T(8,128)S(1)}, f32[8,96]{1,0:T(8,128)S(1)}, u32[]{:S(2)}, u32[]{:S(2)}) collective-permute-start(f32[8,96]{1,0:T(8,128)S(1)} %get-tuple-element.53.refs_0_), channel_id=1, source_target_pairs={{0,24},{4,28},{8,16},{12,20},{16,8},{20,12},{24,0},{28,4},{1,25},{... | collective-permute-start | bytes 9224 | tf_op jit(solution)/shard_map/ppermute | solution.py:379
  54.3 0.0 collective-permute-done.11.refs_2_
  54.3 2.1 %collective-permute-done.12.refs_3_ = f32[8,96]{1,0:T(8,128)S(1)} collective-permute-done((f32[8,96]{1,0:T(8,128)S(1)}, f32[8,96]{1,0:T(8,128)S(1)}, u32[]{:S(2)}, u32[]{:S(2)}) %collective-permute-start.12) | collective-permute-done | bytes 3104 | tf_op jit(solution)/shard_map/ppermute | solution.py:379
  56.4 1.3 %collective-permute-start.13 = (f32[8,96]{1,0:T(8,128)S(1)}, f32[8,96]{1,0:T(8,128)S(1)}, u32[]{:S(2)}, u32[]{:S(2)}) collective-permute-start(f32[8,96]{1,0:T(8,128)S(1)} %get-tuple-element.61.refs_0_), channel_id=1, source_target_pairs={{0,1},{1,2},{2,3},{3,0},{4,5},{5,6},{6,7},{7,4},{8,9},{9,10},{10,1... | collective-permute-start | bytes 9224 | tf_op jit(solution)/shard_map/ppermute | solution.py:332
  57.7 1.1 %collective-permute-start.14 = (f32[8,96]{1,0:T(8,128)S(1)}, f32[8,96]{1,0:T(8,128)S(1)}, u32[]{:S(2)}, u32[]{:S(2)}) collective-permute-start(f32[8,96]{1,0:T(8,128)S(1)} %get-tuple-element.61.refs_0_), channel_id=1, source_target_pairs={{0,2},{1,3},{2,0},{3,1},{4,6},{5,7},{6,4},{7,5},{8,10},{9,11},{10,... | collective-permute-start | bytes 9224 | tf_op jit(solution)/shard_map/ppermute | solution.py:332
  58.8 0.0 collective-permute-done.7.refs_1_
  58.8 2.6 %collective-permute-start.15 = (f32[8,96]{1,0:T(8,128)S(1)}, f32[8,96]{1,0:T(8,128)S(1)}, u32[]{:S(2)}, u32[]{:S(2)}) collective-permute-start(f32[8,96]{1,0:T(8,128)S(1)} %get-tuple-element.61.refs_0_), channel_id=1, source_target_pairs={{0,3},{1,0},{2,1},{3,2},{4,7},{5,4},{6,5},{7,6},{8,11},{9,8},{10,9... | collective-permute-start | bytes 9224 | tf_op jit(solution)/shard_map/ppermute | solution.py:332
  61.4 0.0 collective-permute-done.8.refs_2_
  61.4 0.0 collective-permute-done.9.refs_3_
  61.4 0.9 %shard_map.34 = (bf16[768,384]{1,0:T(8,128)(2,1)S(1)}, bf16[512,16384]{1,0:T(8,128)(2,1)S(1)}, bf16[256,16384]{1,0:T(8,128)(2,1)S(1)}, bf16[384,16384]{1,0:T(8,128)(2,1)S(1)}) custom-call(s32[2]{0:T(128)S(1)} %pad_add_fusion.place_ref, bf16[96,768]{1,0:T(8,128)(2,1)S(1)} %get-tuple-element.52.refs_0_, ...), custom_call_target="tpu_custom_call", output_to_operand_aliasing={{1}: (5, {}), {2}: (6, {}), {3}: (7, {})} | custom-call | tf_op jit(solution)/shard_map/pallas_call | solution.py:249
  62.2 0.0 collective-permute-done.13.refs_1_
  62.3 0.0 collective-permute-done.14.refs_2_
  62.3 0.4 collective-permute-done.15.refs_3_
  62.7 17.6 %shard_map.35 = bf16[768,16384]{1,0:T(8,128)(2,1)} custom-call(s32[2]{0:T(128)S(1)} %pad_add_fusion.place_ref, bf16[768,384]{1,0:T(8,128)(2,1)S(1)} %get-tuple-element.60.across, f32[8,96]{1,0:T(8,128)S(1)} %get-tuple-element.61.refs_0_, f32[8,96]{1,0:T(8,128)S(1)} %collective-permute-done.13.refs_1_, f32[8,96]{1,0:T(8,128)S(1)} %collective-permute-done.14.refs_2_, ...), custom_call_target="tpu_custom_call" | custom-call | tf_op jit(solution)/shard_map/pallas_call | solution.py:315
  (2 shorter events, 0.0 us)
Async XLA Ops:
  19.2 18.2 %collective-permute-start.3 = (s16[112,512]{1,0:T(8,128)(2,1)S(1)}, s16[112,512]{1,0:T(8,128)(2,1)S(1)}, u32[]{:S(2)}, u32[]{:S(2)}) collective-permute-start(s16[112,512]{1,0:T(8,128)(2,1)S(1)} %get-tuple-element.42), channel_id=1, source_target_pairs={{0,1},{1,2},{2,3},{3,0},{4,5},{5,6},{6,7},{7,4},{8,9},{9,10},{10,1... | collective-permute-start | bytes 344072 | tf_op jit(solution)/shard_map/ppermute | solution.py:332
  22.2 17.9 %collective-permute-start.4 = (s16[112,512]{1,0:T(8,128)(2,1)S(1)}, s16[112,512]{1,0:T(8,128)(2,1)S(1)}, u32[]{:S(2)}, u32[]{:S(2)}) collective-permute-start(s16[112,512]{1,0:T(8,128)(2,1)S(1)} %get-tuple-element.43), channel_id=1, source_target_pairs={{0,2},{1,3},{2,0},{3,1},{4,6},{5,7},{6,4},{7,5},{8,10},{9,11},{10,... | collective-permute-start | bytes 344072 | tf_op jit(solution)/shard_map/ppermute | solution.py:332
  24.8 15.4 %collective-permute-start.5 = (s16[112,512]{1,0:T(8,128)(2,1)S(1)}, s16[112,512]{1,0:T(8,128)(2,1)S(1)}, u32[]{:S(2)}, u32[]{:S(2)}) collective-permute-start(s16[112,512]{1,0:T(8,128)(2,1)S(1)} %get-tuple-element.44), channel_id=1, source_target_pairs={{0,3},{1,0},{2,1},{3,2},{4,7},{5,4},{6,5},{7,6},{8,11},{9,8},{10,9... | collective-permute-start | bytes 344072 | tf_op jit(solution)/shard_map/ppermute | solution.py:332
  36.3 6.1 %collective-permute-start = (s16[112,256]{1,0:T(8,128)(2,1)S(1)}, s16[112,256]{1,0:T(8,128)(2,1)S(1)}, u32[]{:S(2)}, u32[]{:S(2)}) collective-permute-start(s16[112,256]{1,0:T(8,128)(2,1)S(1)} %get-tuple-element.38), channel_id=1, source_target_pairs={{0,1},{1,2},{2,3},{3,0},{4,5},{5,6},{6,7},{7,4},{8,9},{9,10},{10,1... | collective-permute-start | bytes 172040 | tf_op jit(solution)/shard_map/ppermute | solution.py:332
  37.0 6.6 %collective-permute-start.1 = (s16[112,256]{1,0:T(8,128)(2,1)S(1)}, s16[112,256]{1,0:T(8,128)(2,1)S(1)}, u32[]{:S(2)}, u32[]{:S(2)}) collective-permute-start(s16[112,256]{1,0:T(8,128)(2,1)S(1)} %get-tuple-element.39), channel_id=1, source_target_pairs={{0,2},{1,3},{2,0},{3,1},{4,6},{5,7},{6,4},{7,5},{8,10},{9,11},{10,... | collective-permute-start | bytes 172040 | tf_op jit(solution)/shard_map/ppermute | solution.py:332
  37.4 6.3 %collective-permute-start.2 = (s16[112,256]{1,0:T(8,128)(2,1)S(1)}, s16[112,256]{1,0:T(8,128)(2,1)S(1)}, u32[]{:S(2)}, u32[]{:S(2)}) collective-permute-start(s16[112,256]{1,0:T(8,128)(2,1)S(1)} %get-tuple-element.40), channel_id=1, source_target_pairs={{0,3},{1,0},{2,1},{3,2},{4,7},{5,4},{6,5},{7,6},{8,11},{9,8},{10,9... | collective-permute-start | bytes 172040 | tf_op jit(solution)/shard_map/ppermute | solution.py:332
  44.2 3.2 %collective-permute-start.6 = (f32[8,96]{1,0:T(8,128)S(1)}, f32[8,96]{1,0:T(8,128)S(1)}, u32[]{:S(2)}, u32[]{:S(2)}) collective-permute-start(f32[8,96]{1,0:T(8,128)S(1)} %get-tuple-element.47.refs_0_.refs_4_), channel_id=1, source_target_pairs={{0,4},{4,0},{8,12},{12,8},{16,20},{20,16},{24,28},{28,24},{1,5},{5... | collective-permute-start | bytes 9224 | tf_op jit(solution)/shard_map/ppermute | solution.py:379
  44.3 14.5 %collective-permute-start.7 = (bf16[96,768]{1,0:T(8,128)(2,1)S(1)}, bf16[96,768]{1,0:T(8,128)(2,1)S(1)}, u32[]{:S(2)}, u32[]{:S(2)}) collective-permute-start(bf16[96,768]{1,0:T(8,128)(2,1)S(1)} %get-tuple-element.48.refs_2_), channel_id=1, source_target_pairs={{0,1},{1,2},{2,3},{3,0},{4,5},{5,6},{6,7},{7,4},{8,9},{9,10},{10,1... | collective-permute-start | bytes 442376 | tf_op jit(solution)/shard_map/ppermute | solution.py:332
  45.6 15.8 %collective-permute-start.8 = (bf16[96,768]{1,0:T(8,128)(2,1)S(1)}, bf16[96,768]{1,0:T(8,128)(2,1)S(1)}, u32[]{:S(2)}, u32[]{:S(2)}) collective-permute-start(bf16[96,768]{1,0:T(8,128)(2,1)S(1)} %get-tuple-element.48.refs_2_), channel_id=1, source_target_pairs={{0,2},{1,3},{2,0},{3,1},{4,6},{5,7},{6,4},{7,5},{8,10},{9,11},{10,... | collective-permute-start | bytes 442376 | tf_op jit(solution)/shard_map/ppermute | solution.py:332
  47.4 14.0 %collective-permute-start.9 = (bf16[96,768]{1,0:T(8,128)(2,1)S(1)}, bf16[96,768]{1,0:T(8,128)(2,1)S(1)}, u32[]{:S(2)}, u32[]{:S(2)}) collective-permute-start(bf16[96,768]{1,0:T(8,128)(2,1)S(1)} %get-tuple-element.52.refs_0_), channel_id=1, source_target_pairs={{0,3},{1,0},{2,1},{3,2},{4,7},{5,4},{6,5},{7,6},{8,11},{9,8},{10,9... | collective-permute-start | bytes 442376 | tf_op jit(solution)/shard_map/ppermute | solution.py:332
  48.2 3.6 %collective-permute-start.10 = (f32[8,96]{1,0:T(8,128)S(1)}, f32[8,96]{1,0:T(8,128)S(1)}, u32[]{:S(2)}, u32[]{:S(2)}) collective-permute-start(f32[8,96]{1,0:T(8,128)S(1)} %get-tuple-element.53.refs_0_), channel_id=1, source_target_pairs={{0,8},{4,12},{8,0},{12,4},{16,24},{20,28},{24,16},{28,20},{1,9},{5... | collective-permute-start | bytes 9224 | tf_op jit(solution)/shard_map/ppermute | solution.py:379
  49.7 4.6 %collective-permute-start.11 = (f32[8,96]{1,0:T(8,128)S(1)}, f32[8,96]{1,0:T(8,128)S(1)}, u32[]{:S(2)}, u32[]{:S(2)}) collective-permute-start(f32[8,96]{1,0:T(8,128)S(1)} %get-tuple-element.53.refs_0_), channel_id=1, source_target_pairs={{0,16},{4,20},{8,24},{12,28},{16,0},{20,4},{24,8},{28,12},{1,17},{... | collective-permute-start | bytes 9224 | tf_op jit(solution)/shard_map/ppermute | solution.py:379
  51.8 4.5 %collective-permute-start.12 = (f32[8,96]{1,0:T(8,128)S(1)}, f32[8,96]{1,0:T(8,128)S(1)}, u32[]{:S(2)}, u32[]{:S(2)}) collective-permute-start(f32[8,96]{1,0:T(8,128)S(1)} %get-tuple-element.53.refs_0_), channel_id=1, source_target_pairs={{0,24},{4,28},{8,16},{12,20},{16,8},{20,12},{24,0},{28,4},{1,25},{... | collective-permute-start | bytes 9224 | tf_op jit(solution)/shard_map/ppermute | solution.py:379
  56.4 5.9 %collective-permute-start.13 = (f32[8,96]{1,0:T(8,128)S(1)}, f32[8,96]{1,0:T(8,128)S(1)}, u32[]{:S(2)}, u32[]{:S(2)}) collective-permute-start(f32[8,96]{1,0:T(8,128)S(1)} %get-tuple-element.61.refs_0_), channel_id=1, source_target_pairs={{0,1},{1,2},{2,3},{3,0},{4,5},{5,6},{6,7},{7,4},{8,9},{9,10},{10,1... | collective-permute-start | bytes 9224 | tf_op jit(solution)/shard_map/ppermute | solution.py:332
  57.7 4.6 %collective-permute-start.14 = (f32[8,96]{1,0:T(8,128)S(1)}, f32[8,96]{1,0:T(8,128)S(1)}, u32[]{:S(2)}, u32[]{:S(2)}) collective-permute-start(f32[8,96]{1,0:T(8,128)S(1)} %get-tuple-element.61.refs_0_), channel_id=1, source_target_pairs={{0,2},{1,3},{2,0},{3,1},{4,6},{5,7},{6,4},{7,5},{8,10},{9,11},{10,... | collective-permute-start | bytes 9224 | tf_op jit(solution)/shard_map/ppermute | solution.py:332
  58.8 3.9 %collective-permute-start.15 = (f32[8,96]{1,0:T(8,128)S(1)}, f32[8,96]{1,0:T(8,128)S(1)}, u32[]{:S(2)}, u32[]{:S(2)}) collective-permute-start(f32[8,96]{1,0:T(8,128)S(1)} %get-tuple-element.61.refs_0_), channel_id=1, source_target_pairs={{0,3},{1,0},{2,1},{3,2},{4,7},{5,4},{6,5},{7,6},{8,11},{9,8},{10,9... | collective-permute-start | bytes 9224 | tf_op jit(solution)/shard_map/ppermute | solution.py:332

commit v6 on v5

--- a/solution.py
+++ b/solution.py
@@ -368,7 +368,12 @@
         [stat, swap(stat, 1, orient_count)], model_a, model_b, counts, weights=weights
     )
     shares = [late] + [shift(weights if k in EARLY else late, k, pix_count) for k in range(1, pix_count)]
-    pairs = [pair] + [swap(pair, k, orient_count) for k in range(2, orient_count, 2)]
+    distance = 2
+    while 2 * distance < orient_count:
+        pairs = [pair, swap(pair, distance, orient_count)]
+        pair, model_a, model_b, counts, stat = merge(pairs, model_a, model_b, counts, weights=stat)
+        distance *= 2
+    pairs = [pair, swap(pair, distance, orient_count)]
     factor, model_a, model_b, counts = merge(pairs, model_a, model_b, counts, stat)
     factors = [factor] + [shift(factor, k, pix_count) for k in range(1, pix_count)]
     across, model_a, model_b, counts = turn(place, shares, model_a, model_b, counts)

time: 80.5 us -> 79.9 us (level)
  starting transfers between devices: 25.3 us -> 22.9 us
  waiting for transfers between devices: 6.14 us -> 7.94 us
    ppermute x4 -> x3, starting transfers between devices: 5.5 us -> 3.12 us  [swap(): return lax.ppermute(x, 'orient', [(i, i ^ distance) for i in range(count)])]
    ppermute x4 -> x3, waiting for transfers between devices: 2.65 us -> 4.19 us  [swap(): return lax.ppermute(x, 'orient', [(i, i ^ distance) for i in range(count)])]
  transfers between devices with their start and end apart: 16 -> 15, of which waited for: 5 -> 5; matrix products, arithmetic and copies ran while one was open for 0% -> 0% of each run, Pallas kernels for 14% -> 14%
where the time goes in v6:
time: 79.9 us; the launch traced here: 79.8 us
  Pallas kernels  48.7 us (61%)
  starting transfers between devices  22.9 us (29%)
  waiting for transfers between devices  7.94 us (10%)
    pallas_call x2, Pallas kernels, partial_scores(): pl.pallas_call(functools.partial(score_kernel, pix_count, beta, first, ro...  29.2 us
    ppermute x12, starting transfers between devices, shift(): return lax.ppermute(x, 'pix', [(i, (i + k) % count) for i in range(count)])  19.8 us
    pallas_call x1, Pallas kernels, update(): pl.pallas_call(functools.partial(update_kernel, len(factors), len(models)...  17.6 us
    ppermute x3, waiting for transfers between devices, swap(): return lax.ppermute(x, 'orient', [(i, i ^ distance) for i in range(count)])  4.19 us
    ppermute x12, waiting for transfers between devices, shift(): return lax.ppermute(x, 'pix', [(i, (i + k) % count) for i in range(count)])  3.75 us
    ppermute x3, starting transfers between devices, swap(): return lax.ppermute(x, 'orient', [(i, i ^ distance) for i in range(count)])  3.12 us
  transfers between devices with their start and end apart: 15, of which 5 were waited for; matrix products, arithmetic and copies ran while one was open for 0% of the time, Pallas kernels for 14%

profile of v6, /device:TPU:0, one launch (start us, length us, event | category | flops | bytes accessed | tf_op | source)
XLA Modules:
  0.0 79.8 jit_solution(3697682252034226498)
XLA Ops:
  0.0 0.1 pad_add_fusion.place_ref
  0.1 19.1 %shard_map.28 = (f32[96,512]{1,0:T(8,128)S(1)}, s16[112,512]{1,0:T(8,128)(2,1)S(1)}, s16[112,512]{1,0:T(8,128)(2,1)S(1)}, s16[112,512]{1,0:T(8,128)(2,1)S(1)}, b...) custom-call(s32[2]{0:T(128)S(1)} %pad_add_fusion.place_ref, bf16[768,16384]{1,0:T(8,128)(2,1)} %model_hbm.3, ...), custom_call_target="tpu_custom_call" | custom-call | tf_op jit(solution)/shard_map/pallas_call | solution.py:184
  19.2 3.1 %collective-permute-start.3 = (s16[112,512]{1,0:T(8,128)(2,1)S(1)}, s16[112,512]{1,0:T(8,128)(2,1)S(1)}, u32[]{:S(2)}, u32[]{:S(2)}) collective-permute-start(s16[112,512]{1,0:T(8,128)(2,1)S(1)} %get-tuple-element.47), channel_id=1, source_target_pairs={{0,1},{1,2},{2,3},{3,0},{4,5},{5,6},{6,7},{7,4},{8,9},{9,10},{10,1... | collective-permute-start | bytes 344072 | tf_op jit(solution)/shard_map/ppermute | solution.py:332
  22.2 2.6 %collective-permute-start.4 = (s16[112,512]{1,0:T(8,128)(2,1)S(1)}, s16[112,512]{1,0:T(8,128)(2,1)S(1)}, u32[]{:S(2)}, u32[]{:S(2)}) collective-permute-start(s16[112,512]{1,0:T(8,128)(2,1)S(1)} %get-tuple-element.48), channel_id=1, source_target_pairs={{0,2},{1,3},{2,0},{3,1},{4,6},{5,7},{6,4},{7,5},{8,10},{9,11},{10,... | collective-permute-start | bytes 344072 | tf_op jit(solution)/shard_map/ppermute | solution.py:332
  24.8 1.3 %collective-permute-start.5 = (s16[112,512]{1,0:T(8,128)(2,1)S(1)}, s16[112,512]{1,0:T(8,128)(2,1)S(1)}, u32[]{:S(2)}, u32[]{:S(2)}) collective-permute-start(s16[112,512]{1,0:T(8,128)(2,1)S(1)} %get-tuple-element.49), channel_id=1, source_target_pairs={{0,3},{1,0},{2,1},{3,2},{4,7},{5,4},{6,5},{7,6},{8,11},{9,8},{10,9... | collective-permute-start | bytes 344072 | tf_op jit(solution)/shard_map/ppermute | solution.py:332
  26.2 10.1 %shard_map.29 = (f32[96,256]{1,0:T(8,128)S(1)}, s16[112,256]{1,0:T(8,128)(2,1)S(1)}, s16[112,256]{1,0:T(8,128)(2,1)S(1)}, s16[112,256]{1,0:T(8,128)(2,1)S(1)}, b...) custom-call(s32[2]{0:T(128)S(1)} %pad_add_fusion.place_ref, ...), custom_call_target="tpu_custom_call", output_to_operand_aliasing={{5}: (3, {})} | custom-call | tf_op jit(solution)/shard_map/pallas_call | solution.py:184
  36.3 0.7 collective-permute-start
  37.0 0.3 collective-permute-start.1
  37.4 0.0 collective-permute-done.3.refs_1_
  37.4 2.8 %collective-permute-start.2 = (s16[112,256]{1,0:T(8,128)(2,1)S(1)}, s16[112,256]{1,0:T(8,128)(2,1)S(1)}, u32[]{:S(2)}, u32[]{:S(2)}) collective-permute-start(s16[112,256]{1,0:T(8,128)(2,1)S(1)} %get-tuple-element.45), channel_id=1, source_target_pairs={{0,3},{1,0},{2,1},{3,2},{4,7},{5,4},{6,5},{7,6},{8,11},{9,8},{10,9... | collective-permute-start | bytes 172040 | tf_op jit(solution)/shard_map/ppermute | solution.py:332
  40.2 0.0 collective-permute-done.4.refs_2_
  40.2 0.0 collective-permute-done.5.refs_3_
  40.2 0.4 shard_map.30.refs_4_
  40.6 1.8 %collective-permute-done.refs_1_ = s16[112,256]{1,0:T(8,128)(2,1)S(1)} collective-permute-done((s16[112,256]{1,0:T(8,128)(2,1)S(1)}, s16[112,256]{1,0:T(8,128)(2,1)S(1)}, u32[]{:S(2)}, u32[]{:S(2)}) %collective-permute-start) | collective-permute-done | bytes 57376 | tf_op jit(solution)/shard_map/ppermute | solution.py:332
  42.4 1.2 %collective-permute-done.1.refs_2_ = s16[112,256]{1,0:T(8,128)(2,1)S(1)} collective-permute-done((s16[112,256]{1,0:T(8,128)(2,1)S(1)}, s16[112,256]{1,0:T(8,128)(2,1)S(1)}, u32[]{:S(2)}, u32[]{:S(2)}) %collective-permute-start.1) | collective-permute-done | bytes 57376 | tf_op jit(solution)/shard_map/ppermute | solution.py:332
  43.7 0.0 collective-permute-done.2.refs_3_
  43.7 0.6 shard_map.31
  44.2 0.0 collective-permute-start.6
  44.3 1.3 %collective-permute-start.7 = (bf16[96,768]{1,0:T(8,128)(2,1)S(1)}, bf16[96,768]{1,0:T(8,128)(2,1)S(1)}, u32[]{:S(2)}, u32[]{:S(2)}) collective-permute-start(bf16[96,768]{1,0:T(8,128)(2,1)S(1)} %get-tuple-element.53.refs_2_), channel_id=1, source_target_pairs={{0,1},{1,2},{2,3},{3,0},{4,5},{5,6},{6,7},{7,4},{8,9},{9,10},{10,1... | collective-permute-start | bytes 442376 | tf_op jit(solution)/shard_map/ppermute | solution.py:332
  45.6 1.8 %collective-permute-start.8 = (bf16[96,768]{1,0:T(8,128)(2,1)S(1)}, bf16[96,768]{1,0:T(8,128)(2,1)S(1)}, u32[]{:S(2)}, u32[]{:S(2)}) collective-permute-start(bf16[96,768]{1,0:T(8,128)(2,1)S(1)} %get-tuple-element.53.refs_2_), channel_id=1, source_target_pairs={{0,2},{1,3},{2,0},{3,1},{4,6},{5,7},{6,4},{7,5},{8,10},{9,11},{10,... | collective-permute-start | bytes 442376 | tf_op jit(solution)/shard_map/ppermute | solution.py:332
  47.4 0.0 collective-permute-done.6.refs_1_
  47.4 0.8 %collective-permute-start.9 = (bf16[96,768]{1,0:T(8,128)(2,1)S(1)}, bf16[96,768]{1,0:T(8,128)(2,1)S(1)}, u32[]{:S(2)}, u32[]{:S(2)}) collective-permute-start(bf16[96,768]{1,0:T(8,128)(2,1)S(1)} %get-tuple-element.57.refs_0_), channel_id=1, source_target_pairs={{0,3},{1,0},{2,1},{3,2},{4,7},{5,4},{6,5},{7,6},{8,11},{9,8},{10,9... | collective-permute-start | bytes 442376 | tf_op jit(solution)/shard_map/ppermute | solution.py:332
  48.2 1.5 %collective-permute-start.10 = (f32[8,96]{1,0:T(8,128)S(1)}, f32[8,96]{1,0:T(8,128)S(1)}, u32[]{:S(2)}, u32[]{:S(2)}) collective-permute-start(f32[8,96]{1,0:T(8,128)S(1)} %get-tuple-element.58.refs_0_), channel_id=1, source_target_pairs={{0,8},{4,12},{8,0},{12,4},{16,24},{20,28},{24,16},{28,20},{1,9},{5... | collective-permute-start | bytes 9224 | tf_op jit(solution)/shard_map/ppermute | solution.py:384
  49.7 2.1 %collective-permute-done.10.refs_1_ = f32[8,96]{1,0:T(8,128)S(1)} collective-permute-done((f32[8,96]{1,0:T(8,128)S(1)}, f32[8,96]{1,0:T(8,128)S(1)}, u32[]{:S(2)}, u32[]{:S(2)}) %collective-permute-start.10) | collective-permute-done | bytes 3104 | tf_op jit(solution)/shard_map/ppermute | solution.py:384
  51.8 1.6 %collective-permute-start.11 = (f32[8,96]{1,0:T(8,128)S(1)}, f32[8,96]{1,0:T(8,128)S(1)}, u32[]{:S(2)}, u32[]{:S(2)}) collective-permute-start(f32[8,96]{1,0:T(8,128)S(1)} %get-tuple-element.62.refs_0_), channel_id=1, source_target_pairs={{0,16},{4,20},{8,24},{12,28},{16,0},{20,4},{24,8},{28,12},{1,17},{... | collective-permute-start | bytes 9224 | tf_op jit(solution)/shard_map/ppermute | solution.py:384
  53.4 2.1 %collective-permute-done.11.refs_1_ = f32[8,96]{1,0:T(8,128)S(1)} collective-permute-done((f32[8,96]{1,0:T(8,128)S(1)}, f32[8,96]{1,0:T(8,128)S(1)}, u32[]{:S(2)}, u32[]{:S(2)}) %collective-permute-start.11) | collective-permute-done | bytes 3104 | tf_op jit(solution)/shard_map/ppermute | solution.py:384
  55.5 1.3 %collective-permute-start.12 = (f32[8,96]{1,0:T(8,128)S(1)}, f32[8,96]{1,0:T(8,128)S(1)}, u32[]{:S(2)}, u32[]{:S(2)}) collective-permute-start(f32[8,96]{1,0:T(8,128)S(1)} %get-tuple-element.71.refs_0_), channel_id=1, source_target_pairs={{0,1},{1,2},{2,3},{3,0},{4,5},{5,6},{6,7},{7,4},{8,9},{9,10},{10,1... | collective-permute-start | bytes 9224 | tf_op jit(solution)/shard_map/ppermute | solution.py:332
  56.8 1.1 %collective-permute-start.13 = (f32[8,96]{1,0:T(8,128)S(1)}, f32[8,96]{1,0:T(8,128)S(1)}, u32[]{:S(2)}, u32[]{:S(2)}) collective-permute-start(f32[8,96]{1,0:T(8,128)S(1)} %get-tuple-element.71.refs_0_), channel_id=1, source_target_pairs={{0,2},{1,3},{2,0},{3,1},{4,6},{5,7},{6,4},{7,5},{8,10},{9,11},{10,... | collective-permute-start | bytes 9224 | tf_op jit(solution)/shard_map/ppermute | solution.py:332
  58.0 0.0 collective-permute-done.7.refs_1_
  58.0 2.6 %collective-permute-start.14 = (f32[8,96]{1,0:T(8,128)S(1)}, f32[8,96]{1,0:T(8,128)S(1)}, u32[]{:S(2)}, u32[]{:S(2)}) collective-permute-start(f32[8,96]{1,0:T(8,128)S(1)} %get-tuple-element.71.refs_0_), channel_id=1, source_target_pairs={{0,3},{1,0},{2,1},{3,2},{4,7},{5,4},{6,5},{7,6},{8,11},{9,8},{10,9... | collective-permute-start | bytes 9224 | tf_op jit(solution)/shard_map/ppermute | solution.py:332
  60.5 0.0 collective-permute-done.8.refs_2_
  60.5 0.0 collective-permute-done.9.refs_3_
  60.5 0.9 %shard_map.35 = (bf16[768,384]{1,0:T(8,128)(2,1)S(1)}, bf16[512,16384]{1,0:T(8,128)(2,1)S(1)}, bf16[256,16384]{1,0:T(8,128)(2,1)S(1)}, bf16[384,16384]{1,0:T(8,128)(2,1)S(1)}) custom-call(s32[2]{0:T(128)S(1)} %pad_add_fusion.place_ref, bf16[96,768]{1,0:T(8,128)(2,1)S(1)} %get-tuple-element.57.refs_0_, ...), custom_call_target="tpu_custom_call", output_to_operand_aliasing={{1}: (5, {}), {2}: (6, {}), {3}: (7, {})} | custom-call | tf_op jit(solution)/shard_map/pallas_call | solution.py:249
  61.4 0.0 collective-permute-done.12.refs_1_
  61.4 0.7 collective-permute-done.13.refs_2_
  62.1 0.0 collective-permute-done.14.refs_3_
  62.1 17.6 %shard_map.36 = bf16[768,16384]{1,0:T(8,128)(2,1)} custom-call(s32[2]{0:T(128)S(1)} %pad_add_fusion.place_ref, bf16[768,384]{1,0:T(8,128)(2,1)S(1)} %get-tuple-element.70.across, f32[8,96]{1,0:T(8,128)S(1)} %get-tuple-element.71.refs_0_, f32[8,96]{1,0:T(8,128)S(1)} %collective-permute-done.12.refs_1_, f32[8,96]{1,0:T(8,128)S(1)} %collective-permute-done.13.refs_2_, ...), custom_call_target="tpu_custom_call" | custom-call | tf_op jit(solution)/shard_map/pallas_call | solution.py:315
  (3 shorter events, 0.0 us)
Async XLA Ops:
  19.2 18.2 %collective-permute-start.3 = (s16[112,512]{1,0:T(8,128)(2,1)S(1)}, s16[112,512]{1,0:T(8,128)(2,1)S(1)}, u32[]{:S(2)}, u32[]{:S(2)}) collective-permute-start(s16[112,512]{1,0:T(8,128)(2,1)S(1)} %get-tuple-element.47), channel_id=1, source_target_pairs={{0,1},{1,2},{2,3},{3,0},{4,5},{5,6},{6,7},{7,4},{8,9},{9,10},{10,1... | collective-permute-start | bytes 344072 | tf_op jit(solution)/shard_map/ppermute | solution.py:332
  22.2 17.9 %collective-permute-start.4 = (s16[112,512]{1,0:T(8,128)(2,1)S(1)}, s16[112,512]{1,0:T(8,128)(2,1)S(1)}, u32[]{:S(2)}, u32[]{:S(2)}) collective-permute-start(s16[112,512]{1,0:T(8,128)(2,1)S(1)} %get-tuple-element.48), channel_id=1, source_target_pairs={{0,2},{1,3},{2,0},{3,1},{4,6},{5,7},{6,4},{7,5},{8,10},{9,11},{10,... | collective-permute-start | bytes 344072 | tf_op jit(solution)/shard_map/ppermute | solution.py:332
  24.8 15.4 %collective-permute-start.5 = (s16[112,512]{1,0:T(8,128)(2,1)S(1)}, s16[112,512]{1,0:T(8,128)(2,1)S(1)}, u32[]{:S(2)}, u32[]{:S(2)}) collective-permute-start(s16[112,512]{1,0:T(8,128)(2,1)S(1)} %get-tuple-element.49), channel_id=1, source_target_pairs={{0,3},{1,0},{2,1},{3,2},{4,7},{5,4},{6,5},{7,6},{8,11},{9,8},{10,9... | collective-permute-start | bytes 344072 | tf_op jit(solution)/shard_map/ppermute | solution.py:332
  36.3 6.1 %collective-permute-start = (s16[112,256]{1,0:T(8,128)(2,1)S(1)}, s16[112,256]{1,0:T(8,128)(2,1)S(1)}, u32[]{:S(2)}, u32[]{:S(2)}) collective-permute-start(s16[112,256]{1,0:T(8,128)(2,1)S(1)} %get-tuple-element.43), channel_id=1, source_target_pairs={{0,1},{1,2},{2,3},{3,0},{4,5},{5,6},{6,7},{7,4},{8,9},{9,10},{10,1... | collective-permute-start | bytes 172040 | tf_op jit(solution)/shard_map/ppermute | solution.py:332
  37.0 6.6 %collective-permute-start.1 = (s16[112,256]{1,0:T(8,128)(2,1)S(1)}, s16[112,256]{1,0:T(8,128)(2,1)S(1)}, u32[]{:S(2)}, u32[]{:S(2)}) collective-permute-start(s16[112,256]{1,0:T(8,128)(2,1)S(1)} %get-tuple-element.44), channel_id=1, source_target_pairs={{0,2},{1,3},{2,0},{3,1},{4,6},{5,7},{6,4},{7,5},{8,10},{9,11},{10,... | collective-permute-start | bytes 172040 | tf_op jit(solution)/shard_map/ppermute | solution.py:332
  37.4 6.3 %collective-permute-start.2 = (s16[112,256]{1,0:T(8,128)(2,1)S(1)}, s16[112,256]{1,0:T(8,128)(2,1)S(1)}, u32[]{:S(2)}, u32[]{:S(2)}) collective-permute-start(s16[112,256]{1,0:T(8,128)(2,1)S(1)} %get-tuple-element.45), channel_id=1, source_target_pairs={{0,3},{1,0},{2,1},{3,2},{4,7},{5,4},{6,5},{7,6},{8,11},{9,8},{10,9... | collective-permute-start | bytes 172040 | tf_op jit(solution)/shard_map/ppermute | solution.py:332
  44.2 3.2 %collective-permute-start.6 = (f32[8,96]{1,0:T(8,128)S(1)}, f32[8,96]{1,0:T(8,128)S(1)}, u32[]{:S(2)}, u32[]{:S(2)}) collective-permute-start(f32[8,96]{1,0:T(8,128)S(1)} %get-tuple-element.52.refs_0_.refs_2_), channel_id=1, source_target_pairs={{0,4},{4,0},{8,12},{12,8},{16,20},{20,16},{24,28},{28,24},{1,5},{5... | collective-permute-start | bytes 9224 | tf_op jit(solution)/shard_map/ppermute | solution.py:384
  44.3 13.7 %collective-permute-start.7 = (bf16[96,768]{1,0:T(8,128)(2,1)S(1)}, bf16[96,768]{1,0:T(8,128)(2,1)S(1)}, u32[]{:S(2)}, u32[]{:S(2)}) collective-permute-start(bf16[96,768]{1,0:T(8,128)(2,1)S(1)} %get-tuple-element.53.refs_2_), channel_id=1, source_target_pairs={{0,1},{1,2},{2,3},{3,0},{4,5},{5,6},{6,7},{7,4},{8,9},{9,10},{10,1... | collective-permute-start | bytes 442376 | tf_op jit(solution)/shard_map/ppermute | solution.py:332
  45.6 15.0 %collective-permute-start.8 = (bf16[96,768]{1,0:T(8,128)(2,1)S(1)}, bf16[96,768]{1,0:T(8,128)(2,1)S(1)}, u32[]{:S(2)}, u32[]{:S(2)}) collective-permute-start(bf16[96,768]{1,0:T(8,128)(2,1)S(1)} %get-tuple-element.53.refs_2_), channel_id=1, source_target_pairs={{0,2},{1,3},{2,0},{3,1},{4,6},{5,7},{6,4},{7,5},{8,10},{9,11},{10,... | collective-permute-start | bytes 442376 | tf_op jit(solution)/shard_map/ppermute | solution.py:332
  47.4 13.1 %collective-permute-start.9 = (bf16[96,768]{1,0:T(8,128)(2,1)S(1)}, bf16[96,768]{1,0:T(8,128)(2,1)S(1)}, u32[]{:S(2)}, u32[]{:S(2)}) collective-permute-start(bf16[96,768]{1,0:T(8,128)(2,1)S(1)} %get-tuple-element.57.refs_0_), channel_id=1, source_target_pairs={{0,3},{1,0},{2,1},{3,2},{4,7},{5,4},{6,5},{7,6},{8,11},{9,8},{10,9... | collective-permute-start | bytes 442376 | tf_op jit(solution)/shard_map/ppermute | solution.py:332
  48.2 3.6 %collective-permute-start.10 = (f32[8,96]{1,0:T(8,128)S(1)}, f32[8,96]{1,0:T(8,128)S(1)}, u32[]{:S(2)}, u32[]{:S(2)}) collective-permute-start(f32[8,96]{1,0:T(8,128)S(1)} %get-tuple-element.58.refs_0_), channel_id=1, source_target_pairs={{0,8},{4,12},{8,0},{12,4},{16,24},{20,28},{24,16},{28,20},{1,9},{5... | collective-permute-start | bytes 9224 | tf_op jit(solution)/shard_map/ppermute | solution.py:384
  51.8 3.7 %collective-permute-start.11 = (f32[8,96]{1,0:T(8,128)S(1)}, f32[8,96]{1,0:T(8,128)S(1)}, u32[]{:S(2)}, u32[]{:S(2)}) collective-permute-start(f32[8,96]{1,0:T(8,128)S(1)} %get-tuple-element.62.refs_0_), channel_id=1, source_target_pairs={{0,16},{4,20},{8,24},{12,28},{16,0},{20,4},{24,8},{28,12},{1,17},{... | collective-permute-start | bytes 9224 | tf_op jit(solution)/shard_map/ppermute | solution.py:384
  55.5 5.9 %collective-permute-start.12 = (f32[8,96]{1,0:T(8,128)S(1)}, f32[8,96]{1,0:T(8,128)S(1)}, u32[]{:S(2)}, u32[]{:S(2)}) collective-permute-start(f32[8,96]{1,0:T(8,128)S(1)} %get-tuple-element.71.refs_0_), channel_id=1, source_target_pairs={{0,1},{1,2},{2,3},{3,0},{4,5},{5,6},{6,7},{7,4},{8,9},{9,10},{10,1... | collective-permute-start | bytes 9224 | tf_op jit(solution)/shard_map/ppermute | solution.py:332
  56.8 5.3 %collective-permute-start.13 = (f32[8,96]{1,0:T(8,128)S(1)}, f32[8,96]{1,0:T(8,128)S(1)}, u32[]{:S(2)}, u32[]{:S(2)}) collective-permute-start(f32[8,96]{1,0:T(8,128)S(1)} %get-tuple-element.71.refs_0_), channel_id=1, source_target_pairs={{0,2},{1,3},{2,0},{3,1},{4,6},{5,7},{6,4},{7,5},{8,10},{9,11},{10,... | collective-permute-start | bytes 9224 | tf_op jit(solution)/shard_map/ppermute | solution.py:332
  58.0 4.1 %collective-permute-start.14 = (f32[8,96]{1,0:T(8,128)S(1)}, f32[8,96]{1,0:T(8,128)S(1)}, u32[]{:S(2)}, u32[]{:S(2)}) collective-permute-start(f32[8,96]{1,0:T(8,128)S(1)} %get-tuple-element.71.refs_0_), channel_id=1, source_target_pairs={{0,3},{1,0},{2,1},{3,2},{4,7},{5,4},{6,5},{7,6},{8,11},{9,8},{10,9... | collective-permute-start | bytes 9224 | tf_op jit(solution)/shard_map/ppermute | solution.py:332
